TPU v7x, 512 devices: a whole 4x8x8 slice. The times are simulated.
512 devices in a mesh: dp: 64 (over z, x, core), mp: 8 (over y).
Axes of the slice: x: 4, y: 8, z: 8, core: 2. Of those that a mesh axis runs over, the one named last changes fastest.
Arguments:
- hidden: bfloat16 [2, 8192, 28672], P(None, 'dp', 'mp'), may hold values from -17 to 17
- cotangent: bfloat16 [2, 8192, 8192], P(None, ('dp', 'mp')), may hold values from -74 to 74
- start_q: float32 [32, 8192], P(None, 'mp'), may hold values from -6 to 6
Outputs:
- factor_q: float32 [32, 8192], P(None, 'mp')
All inputs are finite; a program needn't handle non-finite values.
Results may differ from a plain program's by a relative error of at most 0.014.
Values may be sent and summed in bfloat16 or wider, within the bound.
A program may use at most 64 MiB of HBM per device.

v0:
```python
import jax
import jax.numpy as jnp
from jax import lax
from jax.sharding import PartitionSpec as P

STEPS = 2


def lower_solve(lower_factor, right):
    return lax.linalg.triangular_solve(lower_factor, right, left_side=True, lower=True)


def whole_factor(shard_piece):
    return lax.all_gather(shard_piece, "mp", axis=1, tiled=True)


def on_device(hidden, cotangent, start_q):
    highest = lax.Precision.HIGHEST
    dp_count = lax.axis_size("dp")
    mp_count = lax.axis_size("mp")
    mp_index = lax.axis_index("mp")
    model_width = cotangent.shape[2]
    column_share = model_width // mp_count
    current = whole_factor(start_q)
    all_rows = lax.all_gather(cotangent, "mp", axis=1, tiled=True)
    own_cols = lax.dynamic_slice_in_dim(all_rows, mp_index * column_share, column_share, 2)
    past_p = []
    past_q = []
    result = start_q
    for turn_index in range(STEPS):
        used_steps = turn_index + 1
        qround = current.astype(jnp.bfloat16)
        sketch = jnp.einsum(
            "jtd,rd->jtr", all_rows[:used_steps], qround, preferred_element_type=jnp.float32
        ).astype(jnp.bfloat16)
        partial_value = jnp.einsum(
            "jtr,jtf->rf", sketch, hidden[:used_steps], preferred_element_type=jnp.float32
        )
        factor = lax.psum(partial_value, "dp") / dp_count
        for earlier in range(turn_index):
            weights = jnp.dot(past_q[earlier], current.T, precision=highest)
            factor = factor - jnp.dot(weights.T, past_p[earlier], precision=highest)
        stacked = jnp.stack([factor] + past_p)
        correlations = lax.psum(jnp.einsum("jrf,qf->jrq", stacked, factor, precision=highest), "mp")
        lower_factor = jnp.linalg.cholesky(correlations[0])
        orthonormal = lower_solve(lower_factor, factor)
        pround = orthonormal.astype(jnp.bfloat16)
        projected = jnp.einsum(
            "jtf,rf->jtr", hidden[:used_steps], pround, preferred_element_type=jnp.float32
        )
        mixed_rows = lax.psum(projected, "mp").astype(jnp.bfloat16)
        partial_q = jnp.einsum(
            "jtr,jtc->rc", mixed_rows, own_cols[:used_steps], preferred_element_type=jnp.float32
        )
        update = lax.psum(partial_q, "dp") / dp_count
        for earlier in range(turn_index):
            back_solve = lower_solve(lower_factor, correlations[earlier + 1].T)
            own_past = lax.dynamic_slice_in_dim(
                past_q[earlier], mp_index * column_share, column_share, 1
            )
            update = update - jnp.dot(back_solve, own_past, precision=highest)
        past_p.append(orthonormal)
        if turn_index + 1 < STEPS:
            current = whole_factor(update)
            past_q.append(current)
        else:
            result = update
    return result


def solution(mesh):
    return jax.shard_map(
        on_device,
        mesh=mesh,
        in_specs=(P(None, "dp", "mp"), P(None, ("dp", "mp"), None), P(None, "mp")),
        out_specs=P(None, "mp"),
        check_vma=False,
    )
```

profile of v0, /device:TPU:1, one launch (start us, length us, event | category | flops | bytes accessed | tf_op | source)
XLA Modules:
  0.0 1012.3 jit_solution(17768194861000612455)
XLA Ops:
  8.2 21.7 %all_gather.10 = bf16[32,8192]{1,0:T(8,128)(2,1)S(1)} all-gather(bf16[32,1024]{1,0:T(8,128)(2,1)S(1)} %convert), channel_id=1, replica_groups=mesh['dp'=64,'mp'=8] {'mp'}, dimensions={1}, use_global_device_ids=true | all-gather | bytes 589824 | tf_op jit(solution)/shard_map/all_gather | solution.py:14
  29.9 43.2 %all-gather.3.cloned.1.call-done = bf16[2,128,8192]{2,1,0:T(8,128)(2,1)} async-done(((bf16[2,16,8192]{2,1,0:T(8,128)(2,1)}), bf16[2,128,8192]{2,1,0:T(8,128)(2,1)}) %all-gather.3.cloned.1.call-update) | async-done | bytes 4194320 | tf_op jit(solution)/shard_map/all_gather | solution.py:25
  73.2 3.8 fusion.3
  77.0 189.0 %all-reduce.5.cloned.1.call-done = f32[32,3584]{1,0:T(8,128)} async-done(((f32[32,3584]{1,0:T(8,128)}), f32[32,3584]{1,0:T(8,128)}) %all-reduce.5.cloned.1.call-update) | async-done | bytes 458768 | tf_op jit(solution)/shard_map/psum | solution.py:39
  266.0 1.7 fusion.23
  267.7 22.8 %psum.57 = f32[32,32]{0,1:T(8,128)S(1)} all-reduce(f32[32,32]{0,1:T(8,128)S(1)} %fusion.23), channel_id=1, replica_groups=mesh['dp'=64,'mp'=8] {'mp'}, use_global_device_ids=true, to_apply=%region_1.0 | all-reduce | flops 1024 | bytes 8192 | tf_op jit(solution)/shard_map/psum | solution.py:44
  290.5 2.9 cholesky.44
  294.8 2.4 custom-call.10
  299.2 20.1 %psum.58 = bf16[1,128,32]{1,2,0:T(8,128)(2,1)S(1)} all-reduce(f32[1,128,32]{1,2,0:T(8,128)S(1)} %convolution_bitcast_fusion.3), channel_id=1, replica_groups=mesh['dp'=64,'mp'=8] {'mp'}, use_global_device_ids=true, to_apply=%region_4.7 | all-reduce | flops 4096 | bytes 24576 | tf_op jit(solution)/shard_map/psum | solution.py:51
  319.3 1.8 fusion.25
  321.2 195.1 %all-reduce.7.cloned.1.call-done = f32[32,1024]{1,0:T(8,128)} async-done(((f32[32,1024]{1,0:T(8,128)}), f32[32,1024]{1,0:T(8,128)}) %all-reduce.7.cloned.1.call-update) | async-done | bytes 131088 | tf_op jit(solution)/shard_map/psum | solution.py:55
  517.9 33.3 %all-gather.5.cloned.1.call-done = f32[32,8192]{1,0:T(8,128)} async-done(((f32[32,1024]{1,0:T(8,128)}), f32[32,8192]{1,0:T(8,128)}) %all-gather.5.cloned.1.call-update) | async-done | bytes 1048592 | tf_op jit(solution)/shard_map/all_gather | solution.py:14
  551.2 5.5 convolution_bitcast_fusion
  557.7 192.3 %all-reduce.9.cloned.1.call-done = f32[32,3584]{1,0:T(8,128)} async-done(((f32[32,3584]{1,0:T(8,128)}), f32[32,3584]{1,0:T(8,128)}) %all-reduce.9.cloned.1.call-update) | async-done | bytes 458768 | tf_op jit(solution)/shard_map/psum | solution.py:39
  750.1 1.6 convolution_subtract_fusion
  752.5 2.2 fusion.5
  754.6 22.8 %psum.61 = f32[2,32,32]{1,2,0:T(8,128)S(1)} all-reduce(f32[2,32,32]{1,2,0:T(8,128)S(1)} %fusion.5), channel_id=1, replica_groups=mesh['dp'=64,'mp'=8] {'mp'}, use_global_device_ids=true, to_apply=%region_7.10 | all-reduce | flops 2048 | bytes 16384 | tf_op jit(solution)/shard_map/psum | solution.py:44
  777.5 2.9 cholesky.55
  781.8 2.4 custom-call.11
  784.2 1.6 fusion
  786.4 20.2 %psum.62 = bf16[2,128,32]{1,2,0:T(8,128)(2,1)S(1)} all-reduce(f32[2,128,32]{1,2,0:T(8,128)S(1)} %convolution_bitcast_fusion.2), channel_id=1, replica_groups=mesh['dp'=64,'mp'=8] {'mp'}, use_global_device_ids=true, to_apply=%region_8.11 | all-reduce | flops 8192 | bytes 49152 | tf_op jit(solution)/shard_map/psum | solution.py:51
  806.6 1.9 convolution_bitcast_fusion.1
  808.7 194.9 %all-reduce.11.cloned.1.call-done = f32[32,1024]{1,0:T(8,128)} async-done(((f32[32,1024]{1,0:T(8,128)}), f32[32,1024]{1,0:T(8,128)}) %all-reduce.11.cloned.1.call-update) | async-done | bytes 131088 | tf_op jit(solution)/shard_map/psum | solution.py:55
  1003.6 1.8 convolution_subtract_fusion.1
  (36 shorter events, 10.8 us)
Async XLA Ops:
  6.5 66.6 %all-gather.3.cloned.1.call-start = ((), (), s32[]{:S(2)}) async-start(), calls=%async_computation | async-start | bytes 4718592 | tf_op jit(solution)/shard_map/all_gather | solution.py:25
  7.3 258.8 %all-reduce.5.cloned.1.call-start = ((), (), s32[]{:S(2)}) async-start(), calls=%async_computation.1 | async-start | bytes 917504 | tf_op jit(solution)/shard_map/psum | solution.py:39
  76.9 221.9 %copy-start = (bf16[2,128,3584]{2,1,0:T(8,128)(2,1)S(1)}, bf16[2,128,3584]{2,1,0:T(8,128)(2,1)}, u32[]{:S(2)}) copy-start(bf16[2,128,3584]{2,1,0:T(8,128)(2,1)} %param.6) | copy-start | bytes 5505028
  77.0 439.3 %all-reduce.7.cloned.1.call-start = ((), (), s32[]{:S(2)}) async-start(), calls=%async_computation.2 | async-start | bytes 262144 | tf_op jit(solution)/shard_map/psum | solution.py:55
  321.1 230.0 %all-gather.5.cloned.1.call-start = ((), (), s32[]{:S(2)}) async-start(), calls=%async_computation.3 | async-start | bytes 1179648 | tf_op jit(solution)/shard_map/all_gather | solution.py:14
  517.8 232.2 %all-reduce.9.cloned.1.call-start = ((), (), s32[]{:S(2)}) async-start(), calls=%async_computation.4 | async-start | bytes 917504 | tf_op jit(solution)/shard_map/psum | solution.py:39
  551.2 5.6 copy-start.1
  556.7 446.9 %all-reduce.11.cloned.1.call-start = ((), (), s32[]{:S(2)}) async-start(), calls=%async_computation.5 | async-start | bytes 262144 | tf_op jit(solution)/shard_map/psum | solution.py:55
  751.7 0.8 copy-start.2
Sparse Core Ops, SparseCore 0:
  9.4 63.6 all-gather.2
  77.1 188.8 all-reduce.4
  321.2 194.9 all-reduce.6
  518.2 32.9 all-gather.4
  556.8 193.1 all-reduce.8
  808.6 194.9 all-reduce.10
where the time goes:
time: 1010 us
  waiting for transfers between devices  849 us (84%)
  blocking collectives  108 us (11%)
  matrix products  25.6 us (3%)
  other arithmetic  15.9 us (2%)
  between operations  13.6 us (1%)
    psum x2, waiting for transfers between devices, on_device(): update = lax.psum(partial_q, 'dp') / dp_count  390 us
    psum x2, waiting for transfers between devices, on_device(): factor = lax.psum(partial_value, 'dp') / dp_count  381 us
    psum x2, blocking collectives, on_device(): lax.psum(jnp.einsum('jrf,qf->jrq', stacked, factor, precision=highest), '...  45.5 us
    all_gather x1, waiting for transfers between devices, on_device(): all_rows = lax.all_gather(cotangent, 'mp', axis=1, tiled=True)  43.2 us
    psum x2, blocking collectives, on_device(): mixed_rows = lax.psum(projected, 'mp').astype(jnp.bfloat16)  40.3 us
    all_gather x1, waiting for transfers between devices, whole_factor(): return lax.all_gather(shard_piece, 'mp', axis=1, tiled=True)  33.3 us
    all_gather x1, blocking collectives, whole_factor(): return lax.all_gather(shard_piece, 'mp', axis=1, tiled=True)  21.7 us
  transfers between devices with their start and end apart: 6, of which 6 were waited for; matrix products, arithmetic and copies ran while one was open for 0% of the time, Pallas kernels for 0%

commit v1 on v0

v1 whole, which is shorter than its diff:
```python
import functools

import jax
import jax.numpy as jnp
from jax import lax
from jax.experimental import pallas as pl
from jax.experimental.pallas import tpu as pltpu
from jax.sharding import PartitionSpec as P

MESH = pl.DeviceIdType.MESH
BF = jnp.bfloat16
F32 = jnp.float32
NY = 8
NZ = 8
NX = 4
CHIPS = NZ * NX
TILES = 28
QBLOCKS = 8
HALF = 16
RANK = 32
LANES = 128
Y_ORDER = (4, 3, 5, 2, 6, 1, 7)


def _hops(dz, dx):
    return min(dz, NZ - dz) + min(dx, NX - dx)


ZX_ORDER = sorted(
    [(dz, dx) for dz in range(NZ) for dx in range(NX) if (dz, dx) != (0, 0)],
    key=lambda d: (-_hops(*d), d),
)


def nt_dot(a, b):
    return lax.dot_general(a, b, (((1,), (1,)), ((), ())), preferred_element_type=F32)


def dot(a, b):
    return jnp.dot(a, b, preferred_element_type=F32)


def exact_dot(a, b):
    return jnp.dot(a, b, preferred_element_type=F32, precision=lax.Precision.HIGHEST)


def wait_bytes(ref, sem):
    pltpu.make_async_copy(ref, ref, sem).wait()


def inverse_lower(gram):
    rows = lax.broadcasted_iota(jnp.int32, (RANK, LANES), 0)
    lanes = lax.broadcasted_iota(jnp.int32, (RANK, LANES), 1)
    work = jnp.where(lanes < RANK, gram, jnp.where(lanes == rows + RANK, 1.0, 0.0))
    row_ids = lax.broadcasted_iota(jnp.int32, (RANK, 1), 0)
    scale = jnp.zeros((RANK, 1), F32)
    for j in range(RANK):
        row = work[j : j + 1, :]
        pivot = work[j : j + 1, j : j + 1]
        scale = jnp.where(row_ids == j, pivot, scale)
        if j < RANK - 1:
            factor = jnp.where(row_ids > j, work[:, j : j + 1] / pivot, 0.0)
            work = work - factor * row
    return (work * lax.rsqrt(scale))[:, RANK : 2 * RANK]


def kernel(
    hid, cot, startq, out,
    hbuf, cbuf, tbuf, qf, qsrc, qgat, sk0, sk1, ptsrc, ptrs, pt, mx0, mx1, gram, wbuf,
    zsrc, zrs, zx, qall, qout, minv, umat,
    s_local, s_core, r_core, s_q, r_q, s_sk, r_sk, s_t, r_t, s_tc, r_tc, s_prs, r_prs, s_pag, r_pag,
    s_ptc, r_ptc, s_mx, r_mx, s_g, r_g, s_w, r_w, s_zrs, r_zrs, s_zx, r_zx, s_qag, r_qag,
):
    dp = lax.axis_index("dp")
    y = lax.axis_index("mp")
    c = lax.rem(dp, 2)
    chip = lax.div(dp, 2)
    z = lax.div(chip, NX)
    x = lax.rem(chip, NX)
    sib = {"dp": dp + 1 - 2 * c, "mp": y}

    def y_dev(k):
        return {"dp": dp, "mp": lax.rem(y + k, NY)}

    def zx_chip(dz, dx):
        return lax.rem(z + dz, NZ) * NX + lax.rem(x + dx, NX)

    def zx_dev(there):
        return {"dp": there * 2 + c, "mp": y}

    def send(src, dst, ssem, rsem, dev):
        pltpu.make_async_remote_copy(
            src_ref=src, dst_ref=dst, send_sem=ssem, recv_sem=rsem, device_id=dev, device_id_type=MESH
        ).start()

    load_q = pltpu.make_async_copy(startq, qf, s_local.at[0])
    load_q.start()
    bar = pltpu.get_barrier_semaphore()
    for k in Y_ORDER:
        pl.semaphore_signal(bar, inc=1, device_id=y_dev(k), device_id_type=MESH)
    for d in ZX_ORDER:
        pl.semaphore_signal(bar, inc=1, device_id=zx_dev(zx_chip(*d)), device_id_type=MESH)
    pl.semaphore_signal(bar, inc=1, device_id=sib, device_id_type=MESH)
    load_c = pltpu.make_async_copy(cot.at[0], cbuf.at[c], s_local.at[1])
    load_c.start()
    load_h = [pltpu.make_async_copy(hid.at[j], hbuf.at[j, :, c], s_local.at[2 + j]) for j in range(2)]
    load_h[0].start()
    load_h[1].start()
    load_q.wait()
    qsrc[...] = qf[pl.ds(pl.multiple_of(c * HALF, HALF), HALF), :].astype(BF)
    pl.semaphore_wait(bar, NY - 1 + CHIPS - 1 + 1)

    for n, k in enumerate(Y_ORDER):
        send(qsrc, qgat.at[n], s_q, r_q.at[n], y_dev(k))
    send(cot.at[0], cbuf.at[c], s_core.at[0], r_core.at[0], sib)
    send(hid.at[0], hbuf.at[0, :, c], s_core.at[1], r_core.at[1], sib)
    send(hid.at[1], hbuf.at[1, :, c], s_core.at[2], r_core.at[2], sib)
    load_c.wait()
    wait_bytes(cbuf.at[0], r_core.at[0])

    def block_sketch(q_rows, owner):
        cols = pl.ds(pl.multiple_of(owner * 1024, 1024), 1024)
        return nt_dot(q_rows, cbuf[:, :, cols].reshape(RANK, 1024))

    sketch = block_sketch(qsrc[...], y)
    for n, k in sorted(enumerate(Y_ORDER), key=lambda e: min(e[1], NY - e[1])):
        wait_bytes(qgat.at[n], r_q.at[n])
        sketch = sketch + block_sketch(qgat[n], lax.rem(y - k + NY, NY))
    spot = lax.broadcasted_iota(jnp.int32, (RANK, LANES), 0) + RANK * lax.rem(y, 4)
    place = jnp.where(lax.broadcasted_iota(jnp.int32, (RANK, LANES), 1) == spot, 1.0, 0.0).astype(BF)
    sk0[y] = dot(sketch.astype(BF), place).astype(BF)
    for k in Y_ORDER:
        send(sk0.at[y], sk0.at[y], s_sk.at[0], r_sk.at[0], y_dev(k))
    wait_bytes(sk0.at[pl.ds(0, NY - 1)], r_sk.at[0])

    for j in range(2):
        for k in Y_ORDER:
            there = lax.rem(y + k, NY)
            cols = pl.ds(pl.multiple_of(there * 1024, 1024), 1024)
            send(cot.at[j, :, cols], tbuf.at[j, y, c], s_t.at[j], r_t.at[j], y_dev(k))
        own = pl.ds(pl.multiple_of(y * 1024, 1024), 1024)
        pltpu.make_async_copy(cot.at[j, :, own], tbuf.at[j, y, c], s_local.at[4 + j]).start()

    left = jnp.concatenate(
        [
            (sk0[0] + sk0[1]) + (sk0[2] + sk0[3]),
            (sk0[4] + sk0[5]) + (sk0[6] + sk0[7]),
        ],
        axis=1,
    )

    q_owner = x == lax.rem(z, NX)
    for s in range(2):
        used = s + 1
        for j in range(used):
            if s == j:
                load_h[j].wait()
                wait_bytes(hbuf.at[j, :, 0], r_core.at[1 + j])
        for g in range(4):
            cols = slice(g * 896, (g + 1) * 896)
            part = None
            for j in range(used):
                term = dot(left[:, j * 256 : (j + 1) * 256], hbuf[j, :, :, :, cols].reshape(256, 896))
                part = term if part is None else part + term
            part = part.astype(BF)
            for n in range(7):
                ptsrc[s, g * 7 + n] = part[:, n * LANES : (n + 1) * LANES]
        for d in ZX_ORDER:
            there = zx_chip(*d)

            @pl.when(there < TILES)
            def _(there=there):
                send(ptsrc.at[s, there], ptrs.at[s, chip], s_prs.at[s], r_prs.at[s], zx_dev(there))

        if s == 1:
            wait_bytes(wbuf.at[pl.ds(0, NY - 1)], r_w)
            weights = wbuf[0]
            for n in range(1, NY):
                weights = weights + wbuf[n]
            umat[...] = exact_dot(weights[:, :RANK], minv[0])

        @pl.when(chip < TILES)
        def _():
            ptrs[s, chip] = ptsrc[s, chip]
            wait_bytes(ptrs.at[s, pl.ds(0, CHIPS - 1)], r_prs.at[s])
            total = ptrs[s, 0].astype(F32)
            for n in range(1, CHIPS):
                total = total + ptrs[s, n].astype(F32)
            total = total * (1.0 / 64.0)
            if s == 1:
                past = jnp.concatenate([pt[0, 0, chip], pt[0, 1, chip]], axis=0).astype(F32)
                own_rows = umat[pl.ds(pl.multiple_of(c * HALF, HALF), HALF), :]
                total = total - exact_dot(own_rows, past)
            pt[s, c, chip] = total.astype(BF)
            for d in ZX_ORDER:
                send(pt.at[s, c, chip], pt.at[s, c, chip], s_pag.at[s], r_pag.at[s], zx_dev(zx_chip(*d)))
            wait_bytes(pt.at[s, c, pl.ds(0, TILES - 1)], r_pag.at[s])

        @pl.when(chip >= TILES)
        def _():
            wait_bytes(pt.at[s, c, pl.ds(0, TILES)], r_pag.at[s])

        send(pt.at[s, c], pt.at[s, c], s_ptc.at[s], r_ptc.at[s], sib)

        if s == 0:
            for j in range(2):
                pltpu.make_async_copy(cot.at[j, :, pl.ds(0, 1024)], tbuf.at[j, y, c], s_local.at[4 + j]).wait()
                wait_bytes(tbuf.at[j, pl.ds(0, NY - 1), 0], r_t.at[j])
                send(tbuf.at[j, :, c], tbuf.at[j, :, c], s_tc.at[j], r_tc.at[j], sib)

        mx = mx0 if s == 0 else mx1
        rows = jnp.concatenate([pt[s, c, n] for n in range(TILES)], axis=1)
        for j in range(used):
            mx[y, :, j * 256 : (j + 1) * 256] = nt_dot(rows, hbuf[j].reshape(256, 3584)).astype(BF)
        for k in Y_ORDER:
            send(mx.at[y], mx.at[y], s_mx.at[s], r_mx.at[s], y_dev(k))

        wait_bytes(pt.at[s, 0], r_ptc.at[s])

        def both(step):
            return jnp.concatenate(
                [jnp.concatenate([pt[step, e, n] for n in range(TILES)], axis=1) for e in range(2)], axis=0
            )

        now = both(s)
        other = now if s == 0 else both(0)
        gram[s, y] = nt_dot(now, jnp.concatenate([now, other, now, other], axis=0))
        for k in Y_ORDER:
            send(gram.at[s, y], gram.at[s, y], s_g.at[s], r_g.at[s], y_dev(k))

        wait_bytes(mx.at[pl.ds(0, NY - 1)], r_mx.at[s])
        mixed = mx[0].astype(F32)
        for n in range(1, NY):
            mixed = mixed + mx[n].astype(F32)
        mixed = mixed.astype(BF)

        if s == 0:
            for j in range(2):
                wait_bytes(tbuf.at[j, :, 0], r_tc.at[j])
        part = None
        for j in range(used):
            term = dot(mixed[:, j * 256 : (j + 1) * 256], tbuf[j].reshape(256, 1024))
            part = term if part is None else part + term
        part = part.astype(BF)
        for b in range(QBLOCKS):
            zsrc[s, b] = part[:, b * LANES : (b + 1) * LANES]
        for step in (4, 3, 5, 2, 6, 1, 7, 0):
            b = lax.rem(z + step, NZ)
            there = b * NX + lax.rem(b, NX)

            @pl.when(there != chip)
            def _(b=b, there=there):
                send(zsrc.at[s, b], zrs.at[s, chip], s_zrs.at[s], r_zrs.at[s], zx_dev(there))

        wait_bytes(gram.at[s, pl.ds(0, NY - 1)], r_g.at[s])
        inner = gram[s, 0]
        for n in range(1, NY):
            inner = inner + gram[s, n]
        minv[s] = inverse_lower(inner)
        if s == 1:
            cross = lax.dot_general(
                inner[:, RANK : 2 * RANK], minv[0], (((1,), (1,)), ((), ())),
                preferred_element_type=F32, precision=lax.Precision.HIGHEST,
            )

        dest = qall if s == 0 else qout

        @pl.when(q_owner)
        def _():
            zrs[s, chip] = zsrc[s, z]
            wait_bytes(zrs.at[s, pl.ds(0, CHIPS - 1)], r_zrs.at[s])
            total = zrs[s, 0].astype(F32)
            for n in range(1, CHIPS):
                total = total + zrs[s, n].astype(F32)
            zx[s, c] = total * (1.0 / 64.0)
            send(zx.at[s, c], zx.at[s, c], s_zx.at[s], r_zx.at[s], sib)
            wait_bytes(zx.at[s, 0], r_zx.at[s])
            value = zx[s].reshape(RANK, LANES)
            if s == 1:
                value = value - exact_dot(cross, qall[z].astype(F32))
            dest[z] = exact_dot(minv[s], value).astype(dest.dtype)
            for d in ZX_ORDER:
                send(dest.at[z], dest.at[z], s_qag.at[s], r_qag.at[s], zx_dev(zx_chip(*d)))
            wait_bytes(dest.at[pl.ds(0, QBLOCKS - 1)], r_qag.at[s])

        @pl.when(jnp.logical_not(q_owner))
        def _():
            wait_bytes(dest.at[pl.ds(0, QBLOCKS)], r_qag.at[s])

        if s == 0:
            own_rows = pl.ds(pl.multiple_of(c * HALF, HALF), HALF)
            rows = jnp.concatenate([qall[b, own_rows, :] for b in range(QBLOCKS)], axis=1)
            for j in range(2):
                sk1[y, :, j * 256 : (j + 1) * 256] = nt_dot(rows, tbuf[j].reshape(256, 1024)).astype(BF)
            for k in Y_ORDER:
                send(sk1.at[y], sk1.at[y], s_sk.at[1], r_sk.at[1], y_dev(k))
            whole = jnp.concatenate([qall[b] for b in range(QBLOCKS)], axis=1)
            wbuf[y] = nt_dot(whole, jnp.concatenate([whole] * 4, axis=0))
            for k in Y_ORDER:
                send(wbuf.at[y], wbuf.at[y], s_w, r_w, y_dev(k))
            wait_bytes(sk1.at[pl.ds(0, NY - 1)], r_sk.at[1])
            total = sk1[0].astype(F32)
            for n in range(1, NY):
                total = total + sk1[n].astype(F32)
            left = total.astype(BF)
        else:
            for b in range(QBLOCKS):
                out[:, b * LANES : (b + 1) * LANES] = qout[b].astype(F32)

    wait_bytes(qgat, s_q)
    wait_bytes(cbuf.at[0], s_core.at[0])
    wait_bytes(hbuf.at[0, :, 0], s_core.at[1])
    wait_bytes(hbuf.at[1, :, 0], s_core.at[2])
    wait_bytes(sk0.at[pl.ds(0, NY - 1)], s_sk.at[0])
    wait_bytes(sk1.at[pl.ds(0, NY - 1)], s_sk.at[1])
    wait_bytes(wbuf.at[pl.ds(0, NY - 1)], s_w)
    for s in range(2):
        wait_bytes(tbuf.at[s, pl.ds(0, NY - 1), 0], s_t.at[s])
        wait_bytes(tbuf.at[s, :, 0], s_tc.at[s])
        wait_bytes(pt.at[s, 0], s_ptc.at[s])
        mx = mx0 if s == 0 else mx1
        wait_bytes(mx.at[pl.ds(0, NY - 1)], s_mx.at[s])
        wait_bytes(gram.at[s, pl.ds(0, NY - 1)], s_g.at[s])
        dest = qall if s == 0 else qout

        @pl.when(chip < TILES)
        def _():
            wait_bytes(ptsrc.at[s, pl.ds(0, TILES - 1)], s_prs.at[s])
            wait_bytes(ptrs.at[s, pl.ds(0, CHIPS - 1)], s_pag.at[s])

        @pl.when(chip >= TILES)
        def _():
            wait_bytes(ptsrc.at[s], s_prs.at[s])

        @pl.when(q_owner)
        def _():
            wait_bytes(zsrc.at[s, pl.ds(0, QBLOCKS - 1)], s_zrs.at[s])
            wait_bytes(zx.at[s, 0], s_zx.at[s])
            for _ in range(CHIPS - 1):
                wait_bytes(dest.at[0], s_qag.at[s])

        @pl.when(jnp.logical_not(q_owner))
        def _():
            wait_bytes(zsrc.at[s], s_zrs.at[s])


def on_device(hidden, cotangent, start_q):
    hidden = hidden.reshape(2, NY, 16, 3584)
    dma = pltpu.SemaphoreType.DMA
    vm = pltpu.VMEM
    anywhere = pl.BlockSpec(memory_space=pl.ANY)
    return pl.pallas_call(
        kernel,
        out_shape=jax.ShapeDtypeStruct((RANK, 1024), F32),
        in_specs=[anywhere] * 3,
        out_specs=pl.BlockSpec(memory_space=pltpu.VMEM),
        scratch_shapes=[
            vm((2, NY, 2, 16, 3584), BF),
            vm((2, 16, 8192), BF),
            vm((2, NY, 2, 16, 1024), BF),
            vm((RANK, 1024), F32),
            vm((HALF, 1024), BF),
            vm((NY - 1, HALF, 1024), BF),
            vm((NY, HALF, LANES), BF),
            vm((NY, HALF, 512), BF),
            vm((2, TILES, HALF, LANES), BF),
            vm((2, CHIPS, HALF, LANES), BF),
            vm((2, 2, TILES, HALF, LANES), BF),
            vm((NY, HALF, 256), BF),
            vm((NY, HALF, 512), BF),
            vm((2, NY, RANK, LANES), F32),
            vm((NY, RANK, LANES), F32),
            vm((2, QBLOCKS, HALF, LANES), BF),
            vm((2, CHIPS, HALF, LANES), BF),
            vm((2, 2, HALF, LANES), F32),
            vm((QBLOCKS, RANK, LANES), BF),
            vm((QBLOCKS, RANK, LANES), F32),
            vm((2, RANK, RANK), F32),
            vm((RANK, RANK), F32),
            dma((6,)),
            dma((3,)), dma((3,)),
            dma, dma((NY - 1,)),
            dma((2,)), dma((2,)),
            dma((2,)), dma((2,)),
            dma((2,)), dma((2,)),
            dma((2,)), dma((2,)),
            dma((2,)), dma((2,)),
            dma((2,)), dma((2,)),
            dma((2,)), dma((2,)),
            dma((2,)), dma((2,)),
            dma, dma,
            dma((2,)), dma((2,)),
            dma((2,)), dma((2,)),
            dma((2,)), dma((2,)),
        ],
        compiler_params=pltpu.CompilerParams(
            collective_id=0, has_side_effects=True, vmem_limit_bytes=32 * 1024 * 1024
        ),
        name="powersgd",
    )(hidden, cotangent, start_q)


def solution(mesh):
    return jax.shard_map(
        on_device,
        mesh=mesh,
        in_specs=(P(None, "dp", "mp"), P(None, ("dp", "mp"), None), P(None, "mp")),
        out_specs=P(None, "mp"),
        check_vma=False,
    )
```

time: 1010 us -> 106 us (0.10)
  waiting for transfers between devices: 849 us -> 0 us
  blocking collectives: 108 us -> 0 us
  Pallas kernels: 0 us -> 102 us
  matrix products: 25.6 us -> 0 us
  other arithmetic: 15.9 us -> 0 us
  between operations: 13.6 us -> 0.01 us
    psum x4 -> x0, waiting for transfers between devices: 771 us -> none  [the longest x2 390 us: on_device(): update = lax.psum(partial_q, 'dp') / dp_count]
    pallas_call x0 -> x1, Pallas kernels: none -> 102 us  [on_device(): pl.pallas_call(kernel, out_shape=jax.ShapeDtypeStruct((RANK, 1024), F32),...]
    psum x4 -> x0, blocking collectives: 85.8 us -> none  [the longest x2 45.5 us: on_device(): lax.psum(jnp.einsum('jrf,qf->jrq', stacked, factor, precision=highest), '...]
    all_gather x2 -> x0, waiting for transfers between devices: 76.5 us -> none  [the longest x1 43.2 us: on_device(): all_rows = lax.all_gather(cotangent, 'mp', axis=1, tiled=True)]
    dot_general x11 -> x0, matrix products: 22.1 us -> none  [the longest x2 9.28 us: on_device(): jnp.einsum('jtr,jtf->rf', sketch, hidden[:used_steps], preferred_element_...]
    all_gather x1 -> x0, blocking collectives: 21.7 us -> none  [whole_factor(): return lax.all_gather(shard_piece, 'mp', axis=1, tiled=True)]
    another operation x10 -> x0, other arithmetic: 13.4 us -> none  [the longest x6 7.19 us: on_device(): lower_factor = jnp.linalg.cholesky(correlations[0])]
  transfers between devices with their start and end apart: 6 -> 0, of which waited for: 6 -> 0; matrix products, arithmetic and copies ran while one was open for 0% -> 0% of each run, Pallas kernels for 0% -> 0%
where the time goes in v1:
time: 106 us
  Pallas kernels  102 us (96%)
  local copies, waits for them, and re-layouts  4.1 us (4%)
    pallas_call x1, Pallas kernels, on_device(): pl.pallas_call(kernel, out_shape=jax.ShapeDtypeStruct((RANK, 1024), F32),...  102 us
    unnamed x7, local copies, waits for them, and re-layouts  4.1 us

profile of v1, /device:TPU:1, one launch (start us, length us, event | category | flops | bytes accessed | tf_op | source)
XLA Modules:
  0.0 105.8 jit_solution(16381590273775176999)
XLA Ops:
  0.0 0.0 copy-start
  0.0 1.5 %copy-done = bf16[2,128,3584]{2,1,0:T(8,128)(2,1)S(1)} copy-done((bf16[2,128,3584]{2,1,0:T(8,128)(2,1)S(1)}, bf16[2,128,3584]{2,1,0:T(8,128)(2,1)}, u32[]{:S(2)}) %copy-start) | copy-done | bytes 1835032
  1.5 0.0 copy-start.1
  1.5 1.0 copy-done.1
  2.5 0.0 copy-start.2
  2.5 0.9 copy-done.2
  3.4 101.7 %powersgd.1 = f32[32,1024]{1,0:T(8,128)S(1)} custom-call(bf16[2,8,16,3584]{3,2,1,0:T(8,128)(2,1)S(1)} %bitcast.1, bf16[2,16,8192]{2,1,0:T(8,128)(2,1)S(1)} %copy-done.1, f32[32,1024]{1,0:T(8,128)S(1)} %copy-done.2), custom_call_target="tpu_custom_call" | custom-call | tf_op jit(solution)/shard_map/powersgd/pallas_call | solution.py:352
  105.2 0.7 copy.5
Async XLA Ops:
  0.0 1.5 %copy-start = (bf16[2,128,3584]{2,1,0:T(8,128)(2,1)S(1)}, bf16[2,128,3584]{2,1,0:T(8,128)(2,1)}, u32[]{:S(2)}) copy-start(bf16[2,128,3584]{2,1,0:T(8,128)(2,1)} %param.3) | copy-start | bytes 5505028
  1.5 1.0 copy-start.1
  2.5 0.9 copy-start.2

commit v2 on v1

v2 whole, which is shorter than its diff:
```python
import functools

import jax
import jax.numpy as jnp
from jax import lax
from jax.experimental import pallas as pl
from jax.experimental.pallas import tpu as pltpu
from jax.sharding import PartitionSpec as P

MESH = pl.DeviceIdType.MESH
BF = jnp.bfloat16
F32 = jnp.float32
NY = 8
NZ = 8
NX = 4
CHIPS = NZ * NX
TILES = 28
QBLOCKS = 8
HALF = 16
RANK = 32
LANES = 128
GROUP = 7 * LANES
Y_ORDER = (4, 3, 5, 2, 6, 1, 7)


def _hops(dz, dx):
    return min(dz, NZ - dz) + min(dx, NX - dx)


ZX_ORDER = sorted(
    [(dz, dx) for dz in range(NZ) for dx in range(NX) if (dz, dx) != (0, 0)],
    key=lambda d: (-_hops(*d), d),
)


def nt_dot(a, b):
    return lax.dot_general(a, b, (((1,), (1,)), ((), ())), preferred_element_type=F32)


def dot(a, b):
    return jnp.dot(a, b, preferred_element_type=F32)


def exact_dot(a, b):
    return jnp.dot(a, b, preferred_element_type=F32, precision=lax.Precision.HIGHEST)


def wait_bytes(ref, sem):
    pltpu.make_async_copy(ref, ref, sem).wait()


def exact_nt_dot(a, b):
    return lax.dot_general(
        a, b, (((1,), (1,)), ((), ())), preferred_element_type=F32, precision=lax.Precision.HIGHEST
    )


def pack(value, rows):
    width = LANES * rows // RANK
    lanes = lax.broadcasted_iota(jnp.int32, (rows, LANES), 1)
    packed = value[:rows]
    for k in range(1, RANK // rows):
        packed = jnp.where(lanes >= k * width, value[k * rows : (k + 1) * rows], packed)
    return packed


def unpack(packed):
    rows = packed.shape[0]
    width = LANES * rows // RANK
    return jnp.concatenate(
        [packed] + [pltpu.roll(packed, LANES - k * width, 1) for k in range(1, RANK // rows)], axis=0
    )


def sum_slots(ref, count):
    terms = [ref[n].astype(F32) for n in range(count)]
    while len(terms) > 1:
        terms = [a + b for a, b in zip(terms[::2], terms[1::2])]
    return terms[0]


def inverse_lower(gram):
    rows = lax.broadcasted_iota(jnp.int32, (RANK, LANES), 0)
    lanes = lax.broadcasted_iota(jnp.int32, (RANK, LANES), 1)
    work = jnp.where(lanes < RANK, gram, jnp.where(lanes == rows + RANK, 1.0, 0.0))
    row_ids = lax.broadcasted_iota(jnp.int32, (RANK, 1), 0)
    scale = jnp.zeros((RANK, 1), F32)
    for j in range(RANK):
        row = work[j : j + 1, :]
        pivot = work[j : j + 1, j : j + 1]
        scale = jnp.where(row_ids == j, pivot, scale)
        if j < RANK - 1:
            factor = jnp.where(row_ids > j, work[:, j : j + 1] / pivot, 0.0)
            work = work - factor * row
    return (work * lax.rsqrt(scale))[:, RANK : 2 * RANK]


def kernel(
    hid, cot, startq, out,
    hbuf, cbuf, tbuf, qf, qsrc, qgat, sk0, sk1, ptsrc, ptrs, pt, mx0, mx1, gram0, gram1, wbuf,
    zsrc, zrs, zall, minv, umat,
    s_local, s_core, r_core, s_q, r_q, s_sk, r_sk, s_t, r_t, s_tc, r_tc, s_prs, r_prs, s_pag, r_pag,
    s_ptc, r_ptc, s_mx, r_mx, s_g, r_g, s_w, r_w, s_zrs, r_zrs, s_zx, r_zx, s_qag, r_qag,
):
    dp = lax.axis_index("dp")
    y = lax.axis_index("mp")
    c = lax.rem(dp, 2)
    chip = lax.div(dp, 2)
    z = lax.div(chip, NX)
    x = lax.rem(chip, NX)
    sib = {"dp": dp + 1 - 2 * c, "mp": y}
    pt_owner = z < NZ - 1
    q_owner = lax.rem(x, 2) == lax.rem(z + c, 2)
    ending = []

    def y_dev(k):
        return {"dp": dp, "mp": lax.rem(y + k, NY)}

    def zx_chip(dz, dx):
        return lax.rem(z + dz, NZ) * NX + lax.rem(x + dx, NX)

    def zx_dev(there):
        return {"dp": there * 2 + c, "mp": y}

    def send(src, dst, ssem, rsem, dev):
        pltpu.make_async_remote_copy(
            src_ref=src, dst_ref=dst, send_sem=ssem, recv_sem=rsem, device_id=dev, device_id_type=MESH
        ).start()

    def sent(ref, sem, when=None):
        def wait():
            wait_bytes(ref, sem)

        ending.append(wait if when is None else lambda: pl.when(when)(wait))

    def wait_t1(s):
        if s == 0:
            load_t[1].wait()
            wait_bytes(tbuf.at[1, pl.ds(0, NY - 1), 0], r_t.at[1])

    def wait_t(s):
        if s == 0:
            load_t[0].wait()
            wait_bytes(tbuf.at[0, pl.ds(0, NY - 1), 0], r_t.at[0])
        wait_t1(s)

    def finish():
        for wait in ending:
            wait()

    load_q = pltpu.make_async_copy(startq, qf, s_local.at[0])
    load_q.start()
    bar = pltpu.get_barrier_semaphore()
    for k in Y_ORDER:
        pl.semaphore_signal(bar, inc=1, device_id=y_dev(k), device_id_type=MESH)
    for d in ZX_ORDER:
        pl.semaphore_signal(bar, inc=1, device_id=zx_dev(zx_chip(*d)), device_id_type=MESH)
    pl.semaphore_signal(bar, inc=1, device_id=sib, device_id_type=MESH)
    load_c = pltpu.make_async_copy(cot.at[0], cbuf.at[c], s_local.at[1])
    load_c.start()
    load_h = [pltpu.make_async_copy(hid.at[j], hbuf.at[j, :, c], s_local.at[2 + j]) for j in range(2)]
    load_h[0].start()
    load_h[1].start()
    load_q.wait()
    qsrc[...] = qf[pl.ds(pl.multiple_of(c * HALF, HALF), HALF), :].astype(BF)
    pl.semaphore_wait(bar, NY - 1 + CHIPS - 1 + 1)

    for n, k in enumerate(Y_ORDER):
        send(qsrc, qgat.at[n], s_q, r_q.at[n], y_dev(k))
    sent(qgat, s_q)
    send(cot.at[0], cbuf.at[c], s_core.at[0], r_core.at[0], sib)
    sent(cbuf.at[0], s_core.at[0])
    for j in range(2):
        send(hid.at[j], hbuf.at[j, :, c], s_core.at[1 + j], r_core.at[1 + j], sib)
        sent(hbuf.at[j, :, 0], s_core.at[1 + j])
    load_c.wait()
    wait_bytes(cbuf.at[0], r_core.at[0])

    def block_sketch(q_rows, owner):
        cols = pl.ds(pl.multiple_of(owner * 1024, 1024), 1024)
        return nt_dot(q_rows, cbuf[:, :, cols].reshape(RANK, 1024))

    sketch = block_sketch(qsrc[...], y)
    for n, k in sorted(enumerate(Y_ORDER), key=lambda e: min(e[1], NY - e[1])):
        wait_bytes(qgat.at[n], r_q.at[n])
        sketch = sketch + block_sketch(qgat[n], lax.rem(y - k + NY, NY))
    spot = lax.broadcasted_iota(jnp.int32, (RANK, LANES), 0) + RANK * lax.rem(y, 4)
    place = jnp.where(lax.broadcasted_iota(jnp.int32, (RANK, LANES), 1) == spot, 1.0, 0.0).astype(BF)
    sk0[y] = dot(sketch.astype(BF), place).astype(BF)
    for k in Y_ORDER:
        send(sk0.at[y], sk0.at[y], s_sk.at[0], r_sk.at[0], y_dev(k))
    sent(sk0.at[pl.ds(0, NY - 1)], s_sk.at[0])
    wait_bytes(sk0.at[pl.ds(0, NY - 1)], r_sk.at[0])

    own_cols = pl.ds(pl.multiple_of(y * 1024, 1024), 1024)
    load_t = [pltpu.make_async_copy(cot.at[j, :, own_cols], tbuf.at[j, y, c], s_local.at[4 + j]) for j in range(2)]
    for j in range(2):
        for k in Y_ORDER:
            there = lax.rem(y + k, NY)
            cols = pl.ds(pl.multiple_of(there * 1024, 1024), 1024)
            send(cot.at[j, :, cols], tbuf.at[j, y, c], s_t.at[j], r_t.at[j], y_dev(k))
        sent(tbuf.at[j, pl.ds(0, NY - 1), 0], s_t.at[j])
        load_t[j].start()

    def share_t(j):
        load_t[j].wait()
        wait_bytes(tbuf.at[j, pl.ds(0, NY - 1), 0], r_t.at[j])
        send(tbuf.at[j, :, c], tbuf.at[j, :, c], s_tc.at[j], r_tc.at[j], sib)
        sent(tbuf.at[j, :, 0], s_tc.at[j])

    left = jnp.concatenate(
        [
            (sk0[0] + sk0[1]) + (sk0[2] + sk0[3]),
            (sk0[4] + sk0[5]) + (sk0[6] + sk0[7]),
        ],
        axis=1,
    )

    for s in range(2):
        used = s + 1
        if s == 0:
            load_h[0].wait()
            wait_bytes(hbuf.at[0, :, 0], r_core.at[1])
        for dx in (2, 1, 3, 0):
            g = lax.rem(x + dx, NX)
            cols = pl.ds(pl.multiple_of(g * GROUP, GROUP), GROUP)
            part = None
            for j in range(used):
                term = dot(left[:, j * 256 : (j + 1) * 256], hbuf[j, :, :, :, cols].reshape(256, GROUP))
                part = term if part is None else part + term
            part = part.astype(BF)
            for n in range(7):
                ptsrc[s, g, n] = part[:, n * LANES : (n + 1) * LANES]
            for dz in (4, 3, 5, 2, 6, 1, 7) + ((0,) if dx else ()):
                n = lax.rem(z + dz, NZ)

                @pl.when(n < NZ - 1)
                def _(n=n, g=g):
                    send(ptsrc.at[s, g, n], ptrs.at[s, chip], s_prs.at[s], r_prs.at[s], zx_dev(n * NX + g))

        sent(ptrs.at[s, pl.ds(0, TILES - 1)], s_prs.at[s], pt_owner)
        sent(ptrs.at[s, pl.ds(0, TILES)], s_prs.at[s], jnp.logical_not(pt_owner))

        if s == 0:
            load_h[1].wait()
            wait_bytes(hbuf.at[1, :, 0], r_core.at[2])
        if s == 1:
            wait_bytes(wbuf.at[pl.ds(0, NY - 1)], r_w)
            weights = unpack(sum_slots(wbuf, NY))
            umat[...] = exact_dot(weights[:, :RANK], minv[0])

        @pl.when(pt_owner)
        def _():
            correction = 0.0
            if s == 1:
                past = jnp.concatenate([pt[0, 0, x, z], pt[0, 1, x, z]], axis=0).astype(F32)
                own_rows = umat[pl.ds(pl.multiple_of(c * HALF, HALF), HALF), :]
                correction = exact_dot(own_rows, past)
            ptrs[s, chip] = ptsrc[s, x, z]
            wait_bytes(ptrs.at[s, pl.ds(0, CHIPS - 1)], r_prs.at[s])
            total = sum_slots(ptrs.at[s], CHIPS) * (1.0 / 64.0) - correction
            pt[s, c, x, z] = total.astype(BF)
            for dx in (0, 1, 3, 2):
                for dz in (4, 3, 5, 2, 6, 1, 7) + ((0,) if dx else ()):
                    there = zx_chip(dz, dx)
                    send(pt.at[s, c, x, z], pt.at[s, c, x, z], s_pag.at[s], r_pag.at[s, x], zx_dev(there))

        sent(ptrs.at[s, pl.ds(0, CHIPS - 1)], s_pag.at[s], pt_owner)

        mx = mx0 if s == 0 else mx1
        mixed = [None] * used
        for dx in (0, 1, 3, 2):
            g = lax.rem(x + dx, NX)
            if dx == 0:

                @pl.when(pt_owner)
                def _():
                    wait_bytes(pt.at[s, c, x, pl.ds(0, 6)], r_pag.at[s, x])

                @pl.when(jnp.logical_not(pt_owner))
                def _():
                    wait_bytes(pt.at[s, c, x], r_pag.at[s, x])

            else:
                wait_bytes(pt.at[s, c, g], r_pag.at[s, g])
            cols = pl.ds(pl.multiple_of(g * GROUP, GROUP), GROUP)
            rows = jnp.concatenate([pt[s, c, g, n] for n in range(7)], axis=1)
            for j in range(used):
                term = nt_dot(rows, hbuf[j, :, :, :, cols].reshape(256, GROUP))
                mixed[j] = term if mixed[j] is None else mixed[j] + term
        for j in range(used):
            mx[y, :, j * 256 : (j + 1) * 256] = mixed[j].astype(BF)
        for k in Y_ORDER:
            send(mx.at[y], mx.at[y], s_mx.at[s], r_mx.at[s], y_dev(k))
        sent(mx.at[pl.ds(0, NY - 1)], s_mx.at[s])

        send(pt.at[s, c], pt.at[s, c], s_ptc.at[s], r_ptc.at[s], sib)
        sent(pt.at[s, 0], s_ptc.at[s])
        if s == 0:
            share_t(0)

        wait_bytes(pt.at[s, 0], r_ptc.at[s])

        def both(step):
            return jnp.concatenate(
                [
                    jnp.concatenate([pt[step, e, g, n] for g in range(NX) for n in range(7)], axis=1)
                    for e in range(2)
                ],
                axis=0,
            )

        now = both(s)
        other = now if s == 0 else both(0)
        gram = gram0 if s == 0 else gram1
        gram[y] = pack(nt_dot(now, jnp.concatenate([now, other, now, other], axis=0)), gram.shape[1])
        for k in Y_ORDER:
            send(gram.at[y], gram.at[y], s_g.at[s], r_g.at[s], y_dev(k))
        sent(gram.at[pl.ds(0, NY - 1)], s_g.at[s])

        wait_bytes(mx.at[pl.ds(0, NY - 1)], r_mx.at[s])
        mixed = sum_slots(mx, NY).astype(BF)

        if s == 0:
            wait_bytes(tbuf.at[0, :, 0], r_tc.at[0])
        part = None
        for j in range(used):
            term = dot(mixed[:, j * 256 : (j + 1) * 256], tbuf[j].reshape(256, 1024))
            part = term if part is None else part + term
        for b in range(QBLOCKS):
            zsrc[s, b] = part[:, b * LANES : (b + 1) * LANES]
        for dz in (4, 3, 5, 2, 6, 1, 7, 0):
            b = lax.rem(z + dz, NZ)
            for h in range(2):
                there = b * NX + lax.rem(b + c, 2) + 2 * h

                @pl.when(there != chip)
                def _(b=b, h=h, there=there):
                    send(zsrc.at[s, b, pl.ds(8 * h, 8)], zrs.at[s, chip], s_zrs.at[s], r_zrs.at[s], zx_dev(there))

        sent(zrs.at[s, pl.ds(0, 15)], s_zrs.at[s], q_owner)
        sent(zrs.at[s, pl.ds(0, 16)], s_zrs.at[s], jnp.logical_not(q_owner))
        if s == 0:
            share_t(1)

        wait_bytes(gram.at[pl.ds(0, NY - 1)], r_g.at[s])
        inner = unpack(sum_slots(gram, NY))
        minv[s] = inverse_lower(inner)
        if s == 1:
            cross = lax.dot_general(
                inner[:, RANK : 2 * RANK], minv[0], (((1,), (1,)), ((), ())),
                preferred_element_type=F32, precision=lax.Precision.HIGHEST,
            )
            shift = exact_dot(cross, qf[...])

        @pl.when(q_owner)
        def _():
            mine = pl.ds(pl.multiple_of(8 * lax.div(x, 2), 8), 8)
            zrs[s, chip] = zsrc[s, z, mine, :]
            wait_bytes(zrs.at[s, pl.ds(0, CHIPS - 1)], r_zrs.at[s])
            zall[s, c, z, mine, :] = sum_slots(zrs.at[s], CHIPS) * (1.0 / 64.0)
            for d in ZX_ORDER:
                there = zx_chip(*d)
                send(zall.at[s, c, z, mine], zall.at[s, c, z, mine], s_qag.at[s], r_qag.at[s], zx_dev(there))
            wait_bytes(zrs.at[s, pl.ds(0, 15)], r_qag.at[s])

        sent(zrs.at[s, pl.ds(0, CHIPS - 1)], s_qag.at[s], q_owner)

        @pl.when(jnp.logical_not(q_owner))
        def _():
            wait_bytes(zrs.at[s, pl.ds(0, 16)], r_qag.at[s])

        send(zall.at[s, c], zall.at[s, c], s_zx.at[s], r_zx.at[s], sib)
        sent(zall.at[s, 0], s_zx.at[s])
        wait_bytes(zall.at[s, 0], r_zx.at[s])
        value = jnp.concatenate(
            [jnp.concatenate([zall[s, e, b] for b in range(QBLOCKS)], axis=1) for e in range(2)], axis=0
        )
        if s == 1:
            value = value - shift
        value = exact_dot(minv[s], value)
        if s == 0:
            qf[...] = value
            rows = qf[pl.ds(pl.multiple_of(c * HALF, HALF), HALF), :].astype(BF)
            wait_bytes(tbuf.at[1, :, 0], r_tc.at[1])
            for j in range(2):
                sk1[y, :, j * 256 : (j + 1) * 256] = nt_dot(rows, tbuf[j].reshape(256, 1024)).astype(BF)
            for k in Y_ORDER:
                send(sk1.at[y], sk1.at[y], s_sk.at[1], r_sk.at[1], y_dev(k))
            sent(sk1.at[pl.ds(0, NY - 1)], s_sk.at[1])
            wbuf[y] = pack(exact_nt_dot(value, jnp.concatenate([value] * 4, axis=0)), 8)
            for k in Y_ORDER:
                send(wbuf.at[y], wbuf.at[y], s_w, r_w, y_dev(k))
            sent(wbuf.at[pl.ds(0, NY - 1)], s_w)
            wait_bytes(sk1.at[pl.ds(0, NY - 1)], r_sk.at[1])
            left = sum_slots(sk1, NY).astype(BF)
        else:
            out[...] = value

    finish()


def on_device(hidden, cotangent, start_q):
    hidden = hidden.reshape(2, NY, 16, 3584)
    dma = pltpu.SemaphoreType.DMA
    vm = pltpu.VMEM
    in_hbm = pl.BlockSpec(memory_space=pltpu.HBM)
    return pl.pallas_call(
        kernel,
        out_shape=jax.ShapeDtypeStruct((RANK, 1024), F32),
        in_specs=[in_hbm] * 3,
        out_specs=pl.BlockSpec(memory_space=pltpu.VMEM),
        scratch_shapes=[
            vm((2, NY, 2, 16, 3584), BF),
            vm((2, 16, 8192), BF),
            vm((2, NY, 2, 16, 1024), BF),
            vm((RANK, 1024), F32),
            vm((HALF, 1024), BF),
            vm((NY - 1, HALF, 1024), BF),
            vm((NY, HALF, LANES), BF),
            vm((NY, HALF, 512), BF),
            vm((2, NX, 7, HALF, LANES), BF),
            vm((2, CHIPS, HALF, LANES), BF),
            vm((2, 2, NX, 7, HALF, LANES), BF),
            vm((NY, HALF, 256), BF),
            vm((NY, HALF, 512), BF),
            vm((NY, 8, LANES), F32),
            vm((NY, 16, LANES), F32),
            vm((NY, 8, LANES), F32),
            vm((2, QBLOCKS, HALF, LANES), F32),
            vm((2, CHIPS, 8, LANES), F32),
            vm((2, 2, QBLOCKS, HALF, LANES), F32),
            vm((2, RANK, RANK), F32),
            vm((RANK, RANK), F32),
            dma((6,)),
            dma((3,)), dma((3,)),
            dma, dma((NY - 1,)),
            dma((2,)), dma((2,)),
            dma((2,)), dma((2,)),
            dma((2,)), dma((2,)),
            dma((2,)), dma((2,)),
            dma((2,)), dma((2, NX)),
            dma((2,)), dma((2,)),
            dma((2,)), dma((2,)),
            dma((2,)), dma((2,)),
            dma, dma,
            dma((2,)), dma((2,)),
            dma((2,)), dma((2,)),
            dma((2,)), dma((2,)),
        ],
        compiler_params=pltpu.CompilerParams(
            collective_id=0, has_side_effects=True, vmem_limit_bytes=62 * 1024 * 1024
        ),
        name="powersgd",
    )(hidden, cotangent, start_q)


def solution(mesh):
    return jax.shard_map(
        on_device,
        mesh=mesh,
        in_specs=(P(None, "dp", "mp"), P(None, ("dp", "mp"), None), P(None, "mp")),
        out_specs=P(None, "mp"),
        check_vma=False,
    )
```

time: 106 us -> 103 us (0.972)
  local copies, waits for them, and re-layouts: 4.1 us -> 1.57 us
    unnamed x7 -> x1, local copies, waits for them, and re-layouts: 4.1 us -> 1.57 us
where the time goes in v2:
time: 103 us
  Pallas kernels  101 us (98%)
  local copies, waits for them, and re-layouts  1.57 us (2%)
    pallas_call x1, Pallas kernels, on_device(): pl.pallas_call(kernel, out_shape=jax.ShapeDtypeStruct((RANK, 1024), F32),...  101 us

profile of v2, /device:TPU:1, one launch (start us, length us, event | category | flops | bytes accessed | tf_op | source)
XLA Modules:
  0.0 103.0 jit_solution(1498439203576489303)
XLA Ops:
  0.0 101.4 %powersgd.1 = f32[32,1024]{1,0:T(8,128)} custom-call(bf16[2,8,16,3584]{3,2,1,0:T(8,128)(2,1)} %bitcast.1, bf16[2,16,8192]{2,1,0:T(8,128)(2,1)} %cot.1, f32[32,1024]{1,0:T(8,128)} %startq.1), custom_call_target="tpu_custom_call" | custom-call | tf_op jit(solution)/shard_map/powersgd/pallas_call | solution.py:408
  101.4 1.6 %copy.5 = f32[32,1024]{1,0:T(8,128)} copy(f32[32,1024]{1,0:T(8,128)} %powersgd.1) | data formatting | bytes 262144

commit v3 on v2

--- a/solution.py
+++ b/solution.py
@@ -31,6 +31,7 @@
     [(dz, dx) for dz in range(NZ) for dx in range(NX) if (dz, dx) != (0, 0)],
     key=lambda d: (-_hops(*d), d),
 )
+NEAR_ORDER = [d for d in ZX_ORDER if _hops(*d) < 3 or (_hops(*d) == 3 and d[0] < 4)]
 
 
 def nt_dot(a, b):
@@ -110,7 +111,9 @@
     x = lax.rem(chip, NX)
     sib = {"dp": dp + 1 - 2 * c, "mp": y}
     pt_owner = z < NZ - 1
-    q_owner = lax.rem(x, 2) == lax.rem(z + c, 2)
+    q_side = lax.rem(x + 8 - 2 * c - 2 * lax.div(z, 4), NX)
+    q_owner = q_side < 2
+    q_mine = lax.rem(z, 4) + 4 * lax.rem(q_side, 2)
     ending = []
 
     def y_dev(k):
@@ -133,20 +136,9 @@
 
         ending.append(wait if when is None else lambda: pl.when(when)(wait))
 
-    def wait_t1(s):
-        if s == 0:
-            load_t[1].wait()
-            wait_bytes(tbuf.at[1, pl.ds(0, NY - 1), 0], r_t.at[1])
-
-    def wait_t(s):
-        if s == 0:
-            load_t[0].wait()
-            wait_bytes(tbuf.at[0, pl.ds(0, NY - 1), 0], r_t.at[0])
-        wait_t1(s)
-
     def finish():
-        for wait in ending:
-            wait()
+        while ending:
+            ending.pop(0)()
 
     load_q = pltpu.make_async_copy(startq, qf, s_local.at[0])
     load_q.start()
@@ -194,7 +186,8 @@
 
     own_cols = pl.ds(pl.multiple_of(y * 1024, 1024), 1024)
     load_t = [pltpu.make_async_copy(cot.at[j, :, own_cols], tbuf.at[j, y, c], s_local.at[4 + j]) for j in range(2)]
-    for j in range(2):
+
+    def spread_t(j):
         for k in Y_ORDER:
             there = lax.rem(y + k, NY)
             cols = pl.ds(pl.multiple_of(there * 1024, 1024), 1024)
@@ -221,6 +214,16 @@
         if s == 0:
             load_h[0].wait()
             wait_bytes(hbuf.at[0, :, 0], r_core.at[1])
+        even = lax.rem(z, 2)
+
+        def send_tiles(g, dx, odd):
+            for dz in (4, 2, 6, 0):
+                n = lax.rem(z + dz + odd, NZ)
+
+                @pl.when(jnp.logical_and(n < NZ - 1, n * NX + g != chip))
+                def _(n=n, g=g):
+                    send(ptsrc.at[s, g, n], ptrs.at[s, chip], s_prs.at[s], r_prs.at[s], zx_dev(n * NX + g))
+
         for dx in (2, 1, 3, 0):
             g = lax.rem(x + dx, NX)
             cols = pl.ds(pl.multiple_of(g * GROUP, GROUP), GROUP)
@@ -231,12 +234,11 @@
             part = part.astype(BF)
             for n in range(7):
                 ptsrc[s, g, n] = part[:, n * LANES : (n + 1) * LANES]
-            for dz in (4, 3, 5, 2, 6, 1, 7) + ((0,) if dx else ()):
-                n = lax.rem(z + dz, NZ)
-
-                @pl.when(n < NZ - 1)
-                def _(n=n, g=g):
-                    send(ptsrc.at[s, g, n], ptrs.at[s, chip], s_prs.at[s], r_prs.at[s], zx_dev(n * NX + g))
+            send_tiles(g, dx, even)
+        for dx in (2, 1, 3, 0):
+            send_tiles(lax.rem(x + dx, NX), dx, 1 - even)
+        if s == 0:
+            spread_t(0)
 
         sent(ptrs.at[s, pl.ds(0, TILES - 1)], s_prs.at[s], pt_owner)
         sent(ptrs.at[s, pl.ds(0, TILES)], s_prs.at[s], jnp.logical_not(pt_owner))
@@ -317,6 +319,8 @@
         for k in Y_ORDER:
             send(gram.at[y], gram.at[y], s_g.at[s], r_g.at[s], y_dev(k))
         sent(gram.at[pl.ds(0, NY - 1)], s_g.at[s])
+        if s == 0:
+            spread_t(1)
 
         wait_bytes(mx.at[pl.ds(0, NY - 1)], r_mx.at[s])
         mixed = sum_slots(mx, NY).astype(BF)
@@ -327,21 +331,21 @@
         for j in range(used):
             term = dot(mixed[:, j * 256 : (j + 1) * 256], tbuf[j].reshape(256, 1024))
             part = term if part is None else part + term
+        part = part.astype(BF)
         for b in range(QBLOCKS):
             zsrc[s, b] = part[:, b * LANES : (b + 1) * LANES]
         for dz in (4, 3, 5, 2, 6, 1, 7, 0):
-            b = lax.rem(z + dz, NZ)
+            n = lax.rem(z + dz, NZ)
             for h in range(2):
-                there = b * NX + lax.rem(b + c, 2) + 2 * h
+                b = lax.rem(n, 4) + 4 * h
+                there = n * NX + lax.rem(h + 2 * c + 2 * lax.div(n, 4), NX)
 
                 @pl.when(there != chip)
-                def _(b=b, h=h, there=there):
-                    send(zsrc.at[s, b, pl.ds(8 * h, 8)], zrs.at[s, chip], s_zrs.at[s], r_zrs.at[s], zx_dev(there))
+                def _(b=b, there=there):
+                    send(zsrc.at[s, b], zrs.at[s, chip], s_zrs.at[s], r_zrs.at[s], zx_dev(there))
 
         sent(zrs.at[s, pl.ds(0, 15)], s_zrs.at[s], q_owner)
         sent(zrs.at[s, pl.ds(0, 16)], s_zrs.at[s], jnp.logical_not(q_owner))
-        if s == 0:
-            share_t(1)
 
         wait_bytes(gram.at[pl.ds(0, NY - 1)], r_g.at[s])
         inner = unpack(sum_slots(gram, NY))
@@ -355,20 +359,27 @@
 
         @pl.when(q_owner)
         def _():
-            mine = pl.ds(pl.multiple_of(8 * lax.div(x, 2), 8), 8)
-            zrs[s, chip] = zsrc[s, z, mine, :]
+            zrs[s, chip] = zsrc[s, q_mine]
             wait_bytes(zrs.at[s, pl.ds(0, CHIPS - 1)], r_zrs.at[s])
-            zall[s, c, z, mine, :] = sum_slots(zrs.at[s], CHIPS) * (1.0 / 64.0)
-            for d in ZX_ORDER:
+            zall[s, c, q_mine] = sum_slots(zrs.at[s], CHIPS) * (1.0 / 64.0)
+            for d in NEAR_ORDER:
                 there = zx_chip(*d)
-                send(zall.at[s, c, z, mine], zall.at[s, c, z, mine], s_qag.at[s], r_qag.at[s], zx_dev(there))
-            wait_bytes(zrs.at[s, pl.ds(0, 15)], r_qag.at[s])
-
-        sent(zrs.at[s, pl.ds(0, CHIPS - 1)], s_qag.at[s], q_owner)
+                send(zall.at[s, c, q_mine], zall.at[s, c, q_mine], s_qag.at[s], r_qag.at[s], zx_dev(there))
+
+        sent(zall.at[s, :, pl.ds(0, 7)], s_qag.at[s], q_owner)
+        sent(zall.at[s, 0, 0], s_qag.at[s], q_owner)
+        if s == 0:
+            share_t(1)
+        else:
+            finish()
+
+        @pl.when(q_owner)
+        def _():
+            wait_bytes(zall.at[s, c, pl.ds(0, QBLOCKS - 1)], r_qag.at[s])
 
         @pl.when(jnp.logical_not(q_owner))
         def _():
-            wait_bytes(zrs.at[s, pl.ds(0, 16)], r_qag.at[s])
+            wait_bytes(zall.at[s, c], r_qag.at[s])
 
         send(zall.at[s, c], zall.at[s, c], s_zx.at[s], r_zx.at[s], sib)
         sent(zall.at[s, 0], s_zx.at[s])
@@ -407,7 +418,7 @@
     in_hbm = pl.BlockSpec(memory_space=pltpu.HBM)
     return pl.pallas_call(
         kernel,
-        out_shape=jax.ShapeDtypeStruct((RANK, 1024), F32),
+        out_shape=pltpu.VMEM((RANK, 1024), F32),
         in_specs=[in_hbm] * 3,
         out_specs=pl.BlockSpec(memory_space=pltpu.VMEM),
         scratch_shapes=[
@@ -427,8 +438,8 @@
             vm((NY, 8, LANES), F32),
             vm((NY, 16, LANES), F32),
             vm((NY, 8, LANES), F32),
-            vm((2, QBLOCKS, HALF, LANES), F32),
-            vm((2, CHIPS, 8, LANES), F32),
+            vm((2, QBLOCKS, HALF, LANES), BF),
+            vm((2, CHIPS, HALF, LANES), BF),
             vm((2, 2, QBLOCKS, HALF, LANES), F32),
             vm((2, RANK, RANK), F32),
             vm((RANK, RANK), F32),
@@ -449,7 +460,7 @@
             dma((2,)), dma((2,)),
         ],
         compiler_params=pltpu.CompilerParams(
-            collective_id=0, has_side_effects=True, vmem_limit_bytes=62 * 1024 * 1024
+            collective_id=0, has_side_effects=True, vmem_limit_bytes=56 * 1024 * 1024
         ),
         name="powersgd",
     )(hidden, cotangent, start_q)

time: 103 us -> 99.4 us (0.965)
  Pallas kernels: 101 us -> 98.6 us
    pallas_call x1, Pallas kernels: 101 us -> 98.6 us  [on_device(): pl.pallas_call(kernel, out_shape=pltpu.VMEM((RANK, 1024), F32), in_specs=...]
where the time goes in v3:
time: 99.4 us; the launch traced here: 99.2 us
  Pallas kernels  98.6 us (99%)
    pallas_call x1, Pallas kernels, on_device(): pl.pallas_call(kernel, out_shape=pltpu.VMEM((RANK, 1024), F32), in_specs=...  98.6 us

profile of v3, /device:TPU:1, one launch (start us, length us, event | category | flops | bytes accessed | tf_op | source)
XLA Modules:
  0.0 99.2 jit_solution(5721402405511090607)
XLA Ops:
  0.0 98.6 %powersgd.1 = f32[32,1024]{1,0:T(8,128)S(1)} custom-call(bf16[2,8,16,3584]{3,2,1,0:T(8,128)(2,1)} %bitcast.1, bf16[2,16,8192]{2,1,0:T(8,128)(2,1)} %cot.1, f32[32,1024]{1,0:T(8,128)} %startq.1), custom_call_target="tpu_custom_call" | custom-call | tf_op jit(solution)/shard_map/powersgd/pallas_call | solution.py:419
  98.6 0.7 copy.5

commit v4 on v3

--- a/solution.py
+++ b/solution.py
@@ -98,10 +98,10 @@
 
 def kernel(
     hid, cot, startq, out,
-    hbuf, cbuf, tbuf, qf, qsrc, qgat, sk0, sk1, ptsrc, ptrs, pt, mx0, mx1, gram0, gram1, wbuf,
+    hbuf, cbuf, tbuf, qf, qsrc, qgat, sk0, sk1, ptsrc, ptrs, pt, mx, part0, gram0, gram1, wbuf,
     zsrc, zrs, zall, minv, umat,
     s_local, s_core, r_core, s_q, r_q, s_sk, r_sk, s_t, r_t, s_tc, r_tc, s_prs, r_prs, s_pag, r_pag,
-    s_ptc, r_ptc, s_mx, r_mx, s_g, r_g, s_w, r_w, s_zrs, r_zrs, s_zx, r_zx, s_qag, r_qag,
+    s_ptc, r_ptc, s_mx, r_mx, s_g, r_g, s_w, r_w, s_zrs, r_zrs, s_qag, r_qag,
 ):
     dp = lax.axis_index("dp")
     y = lax.axis_index("mp")
@@ -122,8 +122,8 @@
     def zx_chip(dz, dx):
         return lax.rem(z + dz, NZ) * NX + lax.rem(x + dx, NX)
 
-    def zx_dev(there):
-        return {"dp": there * 2 + c, "mp": y}
+    def zx_dev(there, core=None):
+        return {"dp": there * 2 + (c if core is None else core), "mp": y}
 
     def send(src, dst, ssem, rsem, dev):
         pltpu.make_async_remote_copy(
@@ -147,6 +147,9 @@
         pl.semaphore_signal(bar, inc=1, device_id=y_dev(k), device_id_type=MESH)
     for d in ZX_ORDER:
         pl.semaphore_signal(bar, inc=1, device_id=zx_dev(zx_chip(*d)), device_id_type=MESH)
+    for dz, dx in NEAR_ORDER:
+        back = zx_dev(zx_chip(NZ - dz, NX - dx), 1 - c)
+        pl.semaphore_signal(bar, inc=1, device_id=back, device_id_type=MESH)
     pl.semaphore_signal(bar, inc=1, device_id=sib, device_id_type=MESH)
     load_c = pltpu.make_async_copy(cot.at[0], cbuf.at[c], s_local.at[1])
     load_c.start()
@@ -155,7 +158,7 @@
     load_h[1].start()
     load_q.wait()
     qsrc[...] = qf[pl.ds(pl.multiple_of(c * HALF, HALF), HALF), :].astype(BF)
-    pl.semaphore_wait(bar, NY - 1 + CHIPS - 1 + 1)
+    pl.semaphore_wait(bar, NY - 1 + CHIPS - 1 + len(NEAR_ORDER) + 1)
 
     for n, k in enumerate(Y_ORDER):
         send(qsrc, qgat.at[n], s_q, r_q.at[n], y_dev(k))
@@ -224,13 +227,17 @@
                 def _(n=n, g=g):
                     send(ptsrc.at[s, g, n], ptrs.at[s, chip], s_prs.at[s], r_prs.at[s], zx_dev(n * NX + g))
 
+        if s == 1:
+            wait_bytes(sk1.at[0, pl.ds(0, NY - 1)], r_sk.at[1])
+            part0[...] = dot(sum_slots(sk1.at[0], NY).astype(BF), hbuf[0].reshape(256, 3584))
+            wait_bytes(sk1.at[1, pl.ds(0, NY - 1)], r_sk.at[2])
+            left = sum_slots(sk1.at[1], NY).astype(BF)
         for dx in (2, 1, 3, 0):
             g = lax.rem(x + dx, NX)
             cols = pl.ds(pl.multiple_of(g * GROUP, GROUP), GROUP)
-            part = None
-            for j in range(used):
-                term = dot(left[:, j * 256 : (j + 1) * 256], hbuf[j, :, :, :, cols].reshape(256, GROUP))
-                part = term if part is None else part + term
+            part = dot(left, hbuf[s, :, :, :, cols].reshape(256, GROUP))
+            if s == 1:
+                part = part + part0[:, cols]
             part = part.astype(BF)
             for n in range(7):
                 ptsrc[s, g, n] = part[:, n * LANES : (n + 1) * LANES]
@@ -269,7 +276,6 @@
 
         sent(ptrs.at[s, pl.ds(0, CHIPS - 1)], s_pag.at[s], pt_owner)
 
-        mx = mx0 if s == 0 else mx1
         mixed = [None] * used
         for dx in (0, 1, 3, 2):
             g = lax.rem(x + dx, NX)
@@ -291,10 +297,10 @@
                 term = nt_dot(rows, hbuf[j, :, :, :, cols].reshape(256, GROUP))
                 mixed[j] = term if mixed[j] is None else mixed[j] + term
         for j in range(used):
-            mx[y, :, j * 256 : (j + 1) * 256] = mixed[j].astype(BF)
-        for k in Y_ORDER:
-            send(mx.at[y], mx.at[y], s_mx.at[s], r_mx.at[s], y_dev(k))
-        sent(mx.at[pl.ds(0, NY - 1)], s_mx.at[s])
+            mx[s, j, y] = mixed[j].astype(BF)
+            for k in Y_ORDER:
+                send(mx.at[s, j, y], mx.at[s, j, y], s_mx.at[s, j], r_mx.at[s, j], y_dev(k))
+            sent(mx.at[s, j, pl.ds(0, NY - 1)], s_mx.at[s, j])
 
         send(pt.at[s, c], pt.at[s, c], s_ptc.at[s], r_ptc.at[s], sib)
         sent(pt.at[s, 0], s_ptc.at[s])
@@ -322,14 +328,12 @@
         if s == 0:
             spread_t(1)
 
-        wait_bytes(mx.at[pl.ds(0, NY - 1)], r_mx.at[s])
-        mixed = sum_slots(mx, NY).astype(BF)
-
         if s == 0:
             wait_bytes(tbuf.at[0, :, 0], r_tc.at[0])
         part = None
         for j in range(used):
-            term = dot(mixed[:, j * 256 : (j + 1) * 256], tbuf[j].reshape(256, 1024))
+            wait_bytes(mx.at[s, j, pl.ds(0, NY - 1)], r_mx.at[s, j])
+            term = dot(sum_slots(mx.at[s, j], NY).astype(BF), tbuf[j].reshape(256, 1024))
             part = term if part is None else part + term
         part = part.astype(BF)
         for b in range(QBLOCKS):
@@ -357,17 +361,20 @@
             )
             shift = exact_dot(cross, qf[...])
 
+        z_mine = (2 * s + c) * QBLOCKS + q_mine
+
         @pl.when(q_owner)
         def _():
             zrs[s, chip] = zsrc[s, q_mine]
             wait_bytes(zrs.at[s, pl.ds(0, CHIPS - 1)], r_zrs.at[s])
-            zall[s, c, q_mine] = sum_slots(zrs.at[s], CHIPS) * (1.0 / 64.0)
+            zall[z_mine] = sum_slots(zrs.at[s], CHIPS) * (1.0 / 64.0)
+            tile = zall.at[z_mine]
             for d in NEAR_ORDER:
-                there = zx_chip(*d)
-                send(zall.at[s, c, q_mine], zall.at[s, c, q_mine], s_qag.at[s], r_qag.at[s], zx_dev(there))
-
-        sent(zall.at[s, :, pl.ds(0, 7)], s_qag.at[s], q_owner)
-        sent(zall.at[s, 0, 0], s_qag.at[s], q_owner)
+                for core in (c, 1 - c):
+                    send(tile, tile, s_qag.at[s], r_qag.at[s], zx_dev(zx_chip(*d), core))
+            send(tile, tile, s_qag.at[s], r_qag.at[s], sib)
+
+        sent(zall.at[pl.ds(0, 31)], s_qag.at[s], q_owner)
         if s == 0:
             share_t(1)
         else:
@@ -375,17 +382,18 @@
 
         @pl.when(q_owner)
         def _():
-            wait_bytes(zall.at[s, c, pl.ds(0, QBLOCKS - 1)], r_qag.at[s])
+            wait_bytes(zall.at[pl.ds(0, 15)], r_qag.at[s])
 
         @pl.when(jnp.logical_not(q_owner))
         def _():
-            wait_bytes(zall.at[s, c], r_qag.at[s])
-
-        send(zall.at[s, c], zall.at[s, c], s_zx.at[s], r_zx.at[s], sib)
-        sent(zall.at[s, 0], s_zx.at[s])
-        wait_bytes(zall.at[s, 0], r_zx.at[s])
+            wait_bytes(zall.at[pl.ds(0, 16)], r_qag.at[s])
+
         value = jnp.concatenate(
-            [jnp.concatenate([zall[s, e, b] for b in range(QBLOCKS)], axis=1) for e in range(2)], axis=0
+            [
+                jnp.concatenate([zall[(2 * s + e) * QBLOCKS + b] for b in range(QBLOCKS)], axis=1)
+                for e in range(2)
+            ],
+            axis=0,
         )
         if s == 1:
             value = value - shift
@@ -395,16 +403,14 @@
             rows = qf[pl.ds(pl.multiple_of(c * HALF, HALF), HALF), :].astype(BF)
             wait_bytes(tbuf.at[1, :, 0], r_tc.at[1])
             for j in range(2):
-                sk1[y, :, j * 256 : (j + 1) * 256] = nt_dot(rows, tbuf[j].reshape(256, 1024)).astype(BF)
-            for k in Y_ORDER:
-                send(sk1.at[y], sk1.at[y], s_sk.at[1], r_sk.at[1], y_dev(k))
-            sent(sk1.at[pl.ds(0, NY - 1)], s_sk.at[1])
+                sk1[j, y] = nt_dot(rows, tbuf[j].reshape(256, 1024)).astype(BF)
+                for k in Y_ORDER:
+                    send(sk1.at[j, y], sk1.at[j, y], s_sk.at[1 + j], r_sk.at[1 + j], y_dev(k))
+                sent(sk1.at[j, pl.ds(0, NY - 1)], s_sk.at[1 + j])
             wbuf[y] = pack(exact_nt_dot(value, jnp.concatenate([value] * 4, axis=0)), 8)
             for k in Y_ORDER:
                 send(wbuf.at[y], wbuf.at[y], s_w, r_w, y_dev(k))
             sent(wbuf.at[pl.ds(0, NY - 1)], s_w)
-            wait_bytes(sk1.at[pl.ds(0, NY - 1)], r_sk.at[1])
-            left = sum_slots(sk1, NY).astype(BF)
         else:
             out[...] = value
 
@@ -429,33 +435,32 @@
             vm((HALF, 1024), BF),
             vm((NY - 1, HALF, 1024), BF),
             vm((NY, HALF, LANES), BF),
-            vm((NY, HALF, 512), BF),
+            vm((2, NY, HALF, 256), BF),
             vm((2, NX, 7, HALF, LANES), BF),
             vm((2, CHIPS, HALF, LANES), BF),
             vm((2, 2, NX, 7, HALF, LANES), BF),
-            vm((NY, HALF, 256), BF),
-            vm((NY, HALF, 512), BF),
+            vm((2, 2, NY, HALF, 256), BF),
+            vm((HALF, 3584), F32),
             vm((NY, 8, LANES), F32),
             vm((NY, 16, LANES), F32),
             vm((NY, 8, LANES), F32),
             vm((2, QBLOCKS, HALF, LANES), BF),
             vm((2, CHIPS, HALF, LANES), BF),
-            vm((2, 2, QBLOCKS, HALF, LANES), F32),
+            vm((4 * QBLOCKS, HALF, LANES), F32),
             vm((2, RANK, RANK), F32),
             vm((RANK, RANK), F32),
             dma((6,)),
             dma((3,)), dma((3,)),
             dma, dma((NY - 1,)),
-            dma((2,)), dma((2,)),
+            dma((3,)), dma((3,)),
             dma((2,)), dma((2,)),
             dma((2,)), dma((2,)),
             dma((2,)), dma((2,)),
             dma((2,)), dma((2, NX)),
             dma((2,)), dma((2,)),
-            dma((2,)), dma((2,)),
+            dma((2, 2)), dma((2, 2)),
             dma((2,)), dma((2,)),
             dma, dma,
-            dma((2,)), dma((2,)),
             dma((2,)), dma((2,)),
             dma((2,)), dma((2,)),
         ],

time: 99.4 us -> 97.7 us (0.983)
  Pallas kernels: 98.6 us -> 96.9 us
    pallas_call x1, Pallas kernels: 98.6 us -> 96.9 us  [on_device(): pl.pallas_call(kernel, out_shape=pltpu.VMEM((RANK, 1024), F32), in_specs=...]
where the time goes in v4:
time: 97.7 us; the launch traced here: 97.6 us
  Pallas kernels  96.9 us (99%)
    pallas_call x1, Pallas kernels, on_device(): pl.pallas_call(kernel, out_shape=pltpu.VMEM((RANK, 1024), F32), in_specs=...  96.9 us

profile of v4, /device:TPU:1, one launch (start us, length us, event | category | flops | bytes accessed | tf_op | source)
XLA Modules:
  0.0 97.6 jit_solution(15126373205983895922)
XLA Ops:
  0.0 96.9 %powersgd.1 = f32[32,1024]{1,0:T(8,128)S(1)} custom-call(bf16[2,8,16,3584]{3,2,1,0:T(8,128)(2,1)} %bitcast.1, bf16[2,16,8192]{2,1,0:T(8,128)(2,1)} %cot.1, f32[32,1024]{1,0:T(8,128)} %startq.1), custom_call_target="tpu_custom_call" | custom-call | tf_op jit(solution)/shard_map/powersgd/pallas_call | solution.py:425
  96.9 0.7 copy.5

commit v5 on v4

--- a/solution.py
+++ b/solution.py
@@ -19,7 +19,7 @@
 HALF = 16
 RANK = 32
 LANES = 128
-GROUP = 7 * LANES
+GROUP = NX * LANES
 Y_ORDER = (4, 3, 5, 2, 6, 1, 7)
 
 
@@ -31,7 +31,9 @@
     [(dz, dx) for dz in range(NZ) for dx in range(NX) if (dz, dx) != (0, 0)],
     key=lambda d: (-_hops(*d), d),
 )
-NEAR_ORDER = [d for d in ZX_ORDER if _hops(*d) < 3 or (_hops(*d) == 3 and d[0] < 4)]
+NEAR = ((2, 0), (1, 1), (7, 1), (1, 0), (7, 0), (0, 1), (0, 3), (0, 0))
+PLANES_IN = (0, 1, 6, 2, 5, 3, 4)
+PLANES_OUT = (4, 3, 5, 2, 6, 1, 0)
 
 
 def nt_dot(a, b):
@@ -111,9 +113,7 @@
     x = lax.rem(chip, NX)
     sib = {"dp": dp + 1 - 2 * c, "mp": y}
     pt_owner = z < NZ - 1
-    q_side = lax.rem(x + 8 - 2 * c - 2 * lax.div(z, 4), NX)
-    q_owner = q_side < 2
-    q_mine = lax.rem(z, 4) + 4 * lax.rem(q_side, 2)
+    q_mine = 4 * lax.rem(x, 2) + lax.rem(z + 2 * lax.div(x, 2), 4)
     ending = []
 
     def y_dev(k):
@@ -147,7 +147,7 @@
         pl.semaphore_signal(bar, inc=1, device_id=y_dev(k), device_id_type=MESH)
     for d in ZX_ORDER:
         pl.semaphore_signal(bar, inc=1, device_id=zx_dev(zx_chip(*d)), device_id_type=MESH)
-    for dz, dx in NEAR_ORDER:
+    for dz, dx in NEAR[:-1]:
         back = zx_dev(zx_chip(NZ - dz, NX - dx), 1 - c)
         pl.semaphore_signal(bar, inc=1, device_id=back, device_id_type=MESH)
     pl.semaphore_signal(bar, inc=1, device_id=sib, device_id_type=MESH)
@@ -158,16 +158,13 @@
     load_h[1].start()
     load_q.wait()
     qsrc[...] = qf[pl.ds(pl.multiple_of(c * HALF, HALF), HALF), :].astype(BF)
-    pl.semaphore_wait(bar, NY - 1 + CHIPS - 1 + len(NEAR_ORDER) + 1)
+    pl.semaphore_wait(bar, NY - 1 + CHIPS - 1 + len(NEAR))
 
     for n, k in enumerate(Y_ORDER):
         send(qsrc, qgat.at[n], s_q, r_q.at[n], y_dev(k))
     sent(qgat, s_q)
     send(cot.at[0], cbuf.at[c], s_core.at[0], r_core.at[0], sib)
     sent(cbuf.at[0], s_core.at[0])
-    for j in range(2):
-        send(hid.at[j], hbuf.at[j, :, c], s_core.at[1 + j], r_core.at[1 + j], sib)
-        sent(hbuf.at[j, :, 0], s_core.at[1 + j])
     load_c.wait()
     wait_bytes(cbuf.at[0], r_core.at[0])
 
@@ -185,6 +182,12 @@
     for k in Y_ORDER:
         send(sk0.at[y], sk0.at[y], s_sk.at[0], r_sk.at[0], y_dev(k))
     sent(sk0.at[pl.ds(0, NY - 1)], s_sk.at[0])
+
+    def share_h(j):
+        send(hid.at[j], hbuf.at[j, :, c], s_core.at[1 + j], r_core.at[1 + j], sib)
+        sent(hbuf.at[j, :, 0], s_core.at[1 + j])
+
+    share_h(0)
     wait_bytes(sk0.at[pl.ds(0, NY - 1)], r_sk.at[0])
 
     own_cols = pl.ds(pl.multiple_of(y * 1024, 1024), 1024)
@@ -217,42 +220,39 @@
         if s == 0:
             load_h[0].wait()
             wait_bytes(hbuf.at[0, :, 0], r_core.at[1])
-        even = lax.rem(z, 2)
-
-        def send_tiles(g, dx, odd):
-            for dz in (4, 2, 6, 0):
-                n = lax.rem(z + dz + odd, NZ)
-
-                @pl.when(jnp.logical_and(n < NZ - 1, n * NX + g != chip))
-                def _(n=n, g=g):
-                    send(ptsrc.at[s, g, n], ptrs.at[s, chip], s_prs.at[s], r_prs.at[s], zx_dev(n * NX + g))
-
         if s == 1:
             wait_bytes(sk1.at[0, pl.ds(0, NY - 1)], r_sk.at[1])
             part0[...] = dot(sum_slots(sk1.at[0], NY).astype(BF), hbuf[0].reshape(256, 3584))
+            load_h[1].wait()
+            wait_bytes(hbuf.at[1, :, 0], r_core.at[2])
             wait_bytes(sk1.at[1, pl.ds(0, NY - 1)], r_sk.at[2])
             left = sum_slots(sk1.at[1], NY).astype(BF)
-        for dx in (2, 1, 3, 0):
-            g = lax.rem(x + dx, NX)
-            cols = pl.ds(pl.multiple_of(g * GROUP, GROUP), GROUP)
+        for step in PLANES_OUT:
+            n = lax.rem(z + step, NZ - 1)
+            cols = pl.ds(pl.multiple_of(n * GROUP, GROUP), GROUP)
             part = dot(left, hbuf[s, :, :, :, cols].reshape(256, GROUP))
             if s == 1:
                 part = part + part0[:, cols]
             part = part.astype(BF)
-            for n in range(7):
-                ptsrc[s, g, n] = part[:, n * LANES : (n + 1) * LANES]
-            send_tiles(g, dx, even)
-        for dx in (2, 1, 3, 0):
-            send_tiles(lax.rem(x + dx, NX), dx, 1 - even)
-        if s == 0:
+            for g in range(NX):
+                ptsrc[s, n * NX + g] = part[:, g * LANES : (g + 1) * LANES]
+            for dx in (2, 1, 3, 0):
+                there = n * NX + lax.rem(x + dx, NX)
+
+                def post(there=there):
+                    send(ptsrc.at[s, there], ptrs.at[s, chip], s_prs.at[s], r_prs.at[s], zx_dev(there))
+
+                if step == 0 and dx == 0:
+                    pl.when(jnp.logical_not(pt_owner))(post)
+                else:
+                    post()
+        if s == 0:
+            share_h(1)
             spread_t(0)
 
         sent(ptrs.at[s, pl.ds(0, TILES - 1)], s_prs.at[s], pt_owner)
         sent(ptrs.at[s, pl.ds(0, TILES)], s_prs.at[s], jnp.logical_not(pt_owner))
 
-        if s == 0:
-            load_h[1].wait()
-            wait_bytes(hbuf.at[1, :, 0], r_core.at[2])
         if s == 1:
             wait_bytes(wbuf.at[pl.ds(0, NY - 1)], r_w)
             weights = unpack(sum_slots(wbuf, NY))
@@ -262,37 +262,37 @@
         def _():
             correction = 0.0
             if s == 1:
-                past = jnp.concatenate([pt[0, 0, x, z], pt[0, 1, x, z]], axis=0).astype(F32)
+                past = jnp.concatenate([pt[0, 0, chip], pt[0, 1, chip]], axis=0).astype(F32)
                 own_rows = umat[pl.ds(pl.multiple_of(c * HALF, HALF), HALF), :]
                 correction = exact_dot(own_rows, past)
-            ptrs[s, chip] = ptsrc[s, x, z]
+            ptrs[s, chip] = ptsrc[s, chip]
             wait_bytes(ptrs.at[s, pl.ds(0, CHIPS - 1)], r_prs.at[s])
             total = sum_slots(ptrs.at[s], CHIPS) * (1.0 / 64.0) - correction
-            pt[s, c, x, z] = total.astype(BF)
-            for dx in (0, 1, 3, 2):
-                for dz in (4, 3, 5, 2, 6, 1, 7) + ((0,) if dx else ()):
-                    there = zx_chip(dz, dx)
-                    send(pt.at[s, c, x, z], pt.at[s, c, x, z], s_pag.at[s], r_pag.at[s, x], zx_dev(there))
+            pt[s, c, chip] = total.astype(BF)
+            tile = pt.at[s, c, chip]
+            for d in ZX_ORDER:
+                send(tile, tile, s_pag.at[s], r_pag.at[s, z], zx_dev(zx_chip(*d)))
 
         sent(ptrs.at[s, pl.ds(0, CHIPS - 1)], s_pag.at[s], pt_owner)
 
         mixed = [None] * used
-        for dx in (0, 1, 3, 2):
-            g = lax.rem(x + dx, NX)
-            if dx == 0:
+        for step in PLANES_IN:
+            n = lax.rem(z + step, NZ - 1)
+            first = pl.multiple_of(n * NX, NX)
+            if step == 0:
 
                 @pl.when(pt_owner)
                 def _():
-                    wait_bytes(pt.at[s, c, x, pl.ds(0, 6)], r_pag.at[s, x])
+                    wait_bytes(pt.at[s, c, pl.ds(0, NX - 1)], r_pag.at[s, z])
 
                 @pl.when(jnp.logical_not(pt_owner))
                 def _():
-                    wait_bytes(pt.at[s, c, x], r_pag.at[s, x])
+                    wait_bytes(pt.at[s, c, pl.ds(0, NX)], r_pag.at[s, n])
 
             else:
-                wait_bytes(pt.at[s, c, g], r_pag.at[s, g])
-            cols = pl.ds(pl.multiple_of(g * GROUP, GROUP), GROUP)
-            rows = jnp.concatenate([pt[s, c, g, n] for n in range(7)], axis=1)
+                wait_bytes(pt.at[s, c, pl.ds(0, NX)], r_pag.at[s, n])
+            cols = pl.ds(pl.multiple_of(n * GROUP, GROUP), GROUP)
+            rows = jnp.concatenate([pt[s, c, first + g] for g in range(NX)], axis=1)
             for j in range(used):
                 term = nt_dot(rows, hbuf[j, :, :, :, cols].reshape(256, GROUP))
                 mixed[j] = term if mixed[j] is None else mixed[j] + term
@@ -312,7 +312,7 @@
         def both(step):
             return jnp.concatenate(
                 [
-                    jnp.concatenate([pt[step, e, g, n] for g in range(NX) for n in range(7)], axis=1)
+                    jnp.concatenate([pt[step, e, n] for n in range(TILES)], axis=1)
                     for e in range(2)
                 ],
                 axis=0,
@@ -338,18 +338,11 @@
         part = part.astype(BF)
         for b in range(QBLOCKS):
             zsrc[s, b] = part[:, b * LANES : (b + 1) * LANES]
-        for dz in (4, 3, 5, 2, 6, 1, 7, 0):
-            n = lax.rem(z + dz, NZ)
-            for h in range(2):
-                b = lax.rem(n, 4) + 4 * h
-                there = n * NX + lax.rem(h + 2 * c + 2 * lax.div(n, 4), NX)
-
-                @pl.when(there != chip)
-                def _(b=b, there=there):
-                    send(zsrc.at[s, b], zrs.at[s, chip], s_zrs.at[s], r_zrs.at[s], zx_dev(there))
-
-        sent(zrs.at[s, pl.ds(0, 15)], s_zrs.at[s], q_owner)
-        sent(zrs.at[s, pl.ds(0, 16)], s_zrs.at[s], jnp.logical_not(q_owner))
+        for dz, dx in ZX_ORDER:
+            there = zx_chip(dz, dx)
+            b = 4 * lax.rem(x + dx, 2) + lax.rem(z + dz + 2 * lax.div(lax.rem(x + dx, NX), 2), 4)
+            send(zsrc.at[s, b], zrs.at[s, chip], s_zrs.at[s], r_zrs.at[s], zx_dev(there))
+        sent(zrs.at[s, pl.ds(0, CHIPS - 1)], s_zrs.at[s])
 
         wait_bytes(gram.at[pl.ds(0, NY - 1)], r_g.at[s])
         inner = unpack(sum_slots(gram, NY))
@@ -363,31 +356,19 @@
 
         z_mine = (2 * s + c) * QBLOCKS + q_mine
 
-        @pl.when(q_owner)
-        def _():
-            zrs[s, chip] = zsrc[s, q_mine]
-            wait_bytes(zrs.at[s, pl.ds(0, CHIPS - 1)], r_zrs.at[s])
-            zall[z_mine] = sum_slots(zrs.at[s], CHIPS) * (1.0 / 64.0)
-            tile = zall.at[z_mine]
-            for d in NEAR_ORDER:
-                for core in (c, 1 - c):
-                    send(tile, tile, s_qag.at[s], r_qag.at[s], zx_dev(zx_chip(*d), core))
-            send(tile, tile, s_qag.at[s], r_qag.at[s], sib)
-
-        sent(zall.at[pl.ds(0, 31)], s_qag.at[s], q_owner)
+        zrs[s, chip] = zsrc[s, q_mine]
+        wait_bytes(zrs.at[s, pl.ds(0, CHIPS - 1)], r_zrs.at[s])
+        zall[z_mine] = sum_slots(zrs.at[s], CHIPS) * (1.0 / 64.0)
+        tile = zall.at[z_mine]
+        for d in NEAR:
+            for core in (c, 1 - c) if d != (0, 0) else (1 - c,):
+                send(tile, tile, s_qag.at[s], r_qag.at[s], zx_dev(zx_chip(*d), core))
+        sent(zall.at[pl.ds(0, 15)], s_qag.at[s])
         if s == 0:
             share_t(1)
         else:
             finish()
-
-        @pl.when(q_owner)
-        def _():
-            wait_bytes(zall.at[pl.ds(0, 15)], r_qag.at[s])
-
-        @pl.when(jnp.logical_not(q_owner))
-        def _():
-            wait_bytes(zall.at[pl.ds(0, 16)], r_qag.at[s])
-
+        wait_bytes(zall.at[pl.ds(0, 15)], r_qag.at[s])
         value = jnp.concatenate(
             [
                 jnp.concatenate([zall[(2 * s + e) * QBLOCKS + b] for b in range(QBLOCKS)], axis=1)
@@ -436,9 +417,9 @@
             vm((NY - 1, HALF, 1024), BF),
             vm((NY, HALF, LANES), BF),
             vm((2, NY, HALF, 256), BF),
-            vm((2, NX, 7, HALF, LANES), BF),
+            vm((2, TILES, HALF, LANES), BF),
             vm((2, CHIPS, HALF, LANES), BF),
-            vm((2, 2, NX, 7, HALF, LANES), BF),
+            vm((2, 2, TILES, HALF, LANES), BF),
             vm((2, 2, NY, HALF, 256), BF),
             vm((HALF, 3584), F32),
             vm((NY, 8, LANES), F32),
@@ -456,7 +437,7 @@
             dma((2,)), dma((2,)),
             dma((2,)), dma((2,)),
             dma((2,)), dma((2,)),
-            dma((2,)), dma((2, NX)),
+            dma((2,)), dma((2, NZ - 1)),
             dma((2,)), dma((2,)),
             dma((2, 2)), dma((2, 2)),
             dma((2,)), dma((2,)),

time: 97.7 us -> 95.5 us (0.977)
  Pallas kernels: 96.9 us -> 94.7 us
    pallas_call x1, Pallas kernels: 96.9 us -> 94.7 us  [on_device(): pl.pallas_call(kernel, out_shape=pltpu.VMEM((RANK, 1024), F32), in_specs=...]
where the time goes in v5:
time: 95.5 us; the launch traced here: 95.3 us
  Pallas kernels  94.7 us (99%)
    pallas_call x1, Pallas kernels, on_device(): pl.pallas_call(kernel, out_shape=pltpu.VMEM((RANK, 1024), F32), in_specs=...  94.7 us

profile of v5, /device:TPU:1, one launch (start us, length us, event | category | flops | bytes accessed | tf_op | source)
XLA Modules:
  0.0 95.3 jit_solution(6634338805842709842)
XLA Ops:
  0.0 94.7 %powersgd.1 = f32[32,1024]{1,0:T(8,128)S(1)} custom-call(bf16[2,8,16,3584]{3,2,1,0:T(8,128)(2,1)} %bitcast.1, bf16[2,16,8192]{2,1,0:T(8,128)(2,1)} %cot.1, f32[32,1024]{1,0:T(8,128)} %startq.1), custom_call_target="tpu_custom_call" | custom-call | tf_op jit(solution)/shard_map/powersgd/pallas_call | solution.py:406
  94.7 0.7 copy.5

commit v6 on v5

--- a/solution.py
+++ b/solution.py
@@ -143,14 +143,12 @@
     load_q = pltpu.make_async_copy(startq, qf, s_local.at[0])
     load_q.start()
     bar = pltpu.get_barrier_semaphore()
-    for k in Y_ORDER:
-        pl.semaphore_signal(bar, inc=1, device_id=y_dev(k), device_id_type=MESH)
-    for d in ZX_ORDER:
-        pl.semaphore_signal(bar, inc=1, device_id=zx_dev(zx_chip(*d)), device_id_type=MESH)
-    for dz, dx in NEAR[:-1]:
-        back = zx_dev(zx_chip(NZ - dz, NX - dx), 1 - c)
-        pl.semaphore_signal(bar, inc=1, device_id=back, device_id_type=MESH)
-    pl.semaphore_signal(bar, inc=1, device_id=sib, device_id_type=MESH)
+    greeted = [(_hops(*d), zx_dev(zx_chip(*d))) for d in ZX_ORDER]
+    greeted += [(min(k, NY - k), y_dev(k)) for k in Y_ORDER]
+    greeted += [(_hops(*d), zx_dev(zx_chip(NZ - d[0], NX - d[1]), 1 - c)) for d in NEAR[:-1]]
+    greeted += [(0, sib)]
+    for _, there in sorted(greeted, key=lambda e: -e[0]):
+        pl.semaphore_signal(bar, inc=1, device_id=there, device_id_type=MESH)
     load_c = pltpu.make_async_copy(cot.at[0], cbuf.at[c], s_local.at[1])
     load_c.start()
     load_h = [pltpu.make_async_copy(hid.at[j], hbuf.at[j, :, c], s_local.at[2 + j]) for j in range(2)]
@@ -257,6 +255,9 @@
             wait_bytes(wbuf.at[pl.ds(0, NY - 1)], r_w)
             weights = unpack(sum_slots(wbuf, NY))
             umat[...] = exact_dot(weights[:, :RANK], minv[0])
+            qf[...] = lax.dot_general(
+                minv[0], qf[...], (((0,), (0,)), ((), ())), preferred_element_type=F32, precision=lax.Precision.HIGHEST
+            )
 
         @pl.when(pt_owner)
         def _():
@@ -296,14 +297,14 @@
             for j in range(used):
                 term = nt_dot(rows, hbuf[j, :, :, :, cols].reshape(256, GROUP))
                 mixed[j] = term if mixed[j] is None else mixed[j] + term
+        send(pt.at[s, c], pt.at[s, c], s_ptc.at[s], r_ptc.at[s], sib)
+        sent(pt.at[s, 0], s_ptc.at[s])
         for j in range(used):
             mx[s, j, y] = mixed[j].astype(BF)
             for k in Y_ORDER:
                 send(mx.at[s, j, y], mx.at[s, j, y], s_mx.at[s, j], r_mx.at[s, j], y_dev(k))
             sent(mx.at[s, j, pl.ds(0, NY - 1)], s_mx.at[s, j])
 
-        send(pt.at[s, c], pt.at[s, c], s_ptc.at[s], r_ptc.at[s], sib)
-        sent(pt.at[s, 0], s_ptc.at[s])
         if s == 0:
             share_t(0)
 
@@ -344,15 +345,11 @@
             send(zsrc.at[s, b], zrs.at[s, chip], s_zrs.at[s], r_zrs.at[s], zx_dev(there))
         sent(zrs.at[s, pl.ds(0, CHIPS - 1)], s_zrs.at[s])
 
-        wait_bytes(gram.at[pl.ds(0, NY - 1)], r_g.at[s])
-        inner = unpack(sum_slots(gram, NY))
-        minv[s] = inverse_lower(inner)
-        if s == 1:
-            cross = lax.dot_general(
-                inner[:, RANK : 2 * RANK], minv[0], (((1,), (1,)), ((), ())),
-                preferred_element_type=F32, precision=lax.Precision.HIGHEST,
-            )
-            shift = exact_dot(cross, qf[...])
+        if s == 0:
+            share_t(1)
+        else:
+            finish()
+
 
         z_mine = (2 * s + c) * QBLOCKS + q_mine
 
@@ -364,10 +361,12 @@
             for core in (c, 1 - c) if d != (0, 0) else (1 - c,):
                 send(tile, tile, s_qag.at[s], r_qag.at[s], zx_dev(zx_chip(*d), core))
         sent(zall.at[pl.ds(0, 15)], s_qag.at[s])
-        if s == 0:
-            share_t(1)
-        else:
-            finish()
+
+        wait_bytes(gram.at[pl.ds(0, NY - 1)], r_g.at[s])
+        inner = unpack(sum_slots(gram, NY))
+        if s == 1:
+            shift = exact_dot(inner[:, RANK : 2 * RANK], qf[...])
+        minv[s] = inverse_lower(inner)
         wait_bytes(zall.at[pl.ds(0, 15)], r_qag.at[s])
         value = jnp.concatenate(
             [

time: 95.5 us -> 95.2 us (level)
  no operation moved by 1% of the time
where the time goes in v6:
time: 95.2 us; the launch traced here: 95 us
  Pallas kernels  94.4 us (99%)
    pallas_call x1, Pallas kernels, on_device(): pl.pallas_call(kernel, out_shape=pltpu.VMEM((RANK, 1024), F32), in_specs=...  94.4 us

profile of v6, /device:TPU:1, one launch (start us, length us, event | category | flops | bytes accessed | tf_op | source)
XLA Modules:
  0.0 95.0 jit_solution(18367309674168172966)
XLA Ops:
  0.0 94.4 %powersgd.1 = f32[32,1024]{1,0:T(8,128)S(1)} custom-call(bf16[2,8,16,3584]{3,2,1,0:T(8,128)(2,1)} %bitcast.1, bf16[2,16,8192]{2,1,0:T(8,128)(2,1)} %cot.1, f32[32,1024]{1,0:T(8,128)} %startq.1), custom_call_target="tpu_custom_call" | custom-call | tf_op jit(solution)/shard_map/powersgd/pallas_call | solution.py:405
  94.4 0.7 copy.5

commit v7 on v6

--- a/solution.py
+++ b/solution.py
@@ -101,7 +101,7 @@
 def kernel(
     hid, cot, startq, out,
     hbuf, cbuf, tbuf, qf, qsrc, qgat, sk0, sk1, ptsrc, ptrs, pt, mx, part0, gram0, gram1, wbuf,
-    zsrc, zrs, zall, minv, umat,
+    zsrc, zrs, zall, mparts, shifted, minv, umat,
     s_local, s_core, r_core, s_q, r_q, s_sk, r_sk, s_t, r_t, s_tc, r_tc, s_prs, r_prs, s_pag, r_pag,
     s_ptc, r_ptc, s_mx, r_mx, s_g, r_g, s_w, r_w, s_zrs, r_zrs, s_qag, r_qag,
 ):
@@ -345,28 +345,33 @@
             send(zsrc.at[s, b], zrs.at[s, chip], s_zrs.at[s], r_zrs.at[s], zx_dev(there))
         sent(zrs.at[s, pl.ds(0, CHIPS - 1)], s_zrs.at[s])
 
-        if s == 0:
-            share_t(1)
-        else:
-            finish()
+        wait_bytes(gram.at[pl.ds(0, NY - 1)], r_g.at[s])
+        inner = unpack(sum_slots(gram, NY))
+        minv[s] = inverse_lower(inner)
+        rest = minv[s]
+        for n in range(3):
+            part = rest.astype(BF)
+            mparts[n * RANK : (n + 1) * RANK, :] = part
+            rest = rest - part.astype(F32)
+        if s == 1:
+            shifted[...] = exact_dot(minv[1], exact_dot(inner[:, RANK : 2 * RANK], qf[...]))
 
 
         z_mine = (2 * s + c) * QBLOCKS + q_mine
 
         zrs[s, chip] = zsrc[s, q_mine]
         wait_bytes(zrs.at[s, pl.ds(0, CHIPS - 1)], r_zrs.at[s])
-        zall[z_mine] = sum_slots(zrs.at[s], CHIPS) * (1.0 / 64.0)
+        zall[z_mine] = (sum_slots(zrs.at[s], CHIPS) * (1.0 / 64.0)).astype(BF)
         tile = zall.at[z_mine]
         for d in NEAR:
             for core in (c, 1 - c) if d != (0, 0) else (1 - c,):
                 send(tile, tile, s_qag.at[s], r_qag.at[s], zx_dev(zx_chip(*d), core))
         sent(zall.at[pl.ds(0, 15)], s_qag.at[s])
 
-        wait_bytes(gram.at[pl.ds(0, NY - 1)], r_g.at[s])
-        inner = unpack(sum_slots(gram, NY))
-        if s == 1:
-            shift = exact_dot(inner[:, RANK : 2 * RANK], qf[...])
-        minv[s] = inverse_lower(inner)
+        if s == 0:
+            share_t(1)
+        else:
+            finish()
         wait_bytes(zall.at[pl.ds(0, 15)], r_qag.at[s])
         value = jnp.concatenate(
             [
@@ -375,9 +380,10 @@
             ],
             axis=0,
         )
+        parts = dot(mparts[...], value)
+        value = parts[:RANK] + (parts[RANK : 2 * RANK] + parts[2 * RANK :])
         if s == 1:
-            value = value - shift
-        value = exact_dot(minv[s], value)
+            value = value - shifted[...]
         if s == 0:
             qf[...] = value
             rows = qf[pl.ds(pl.multiple_of(c * HALF, HALF), HALF), :].astype(BF)
@@ -426,7 +432,9 @@
             vm((NY, 8, LANES), F32),
             vm((2, QBLOCKS, HALF, LANES), BF),
             vm((2, CHIPS, HALF, LANES), BF),
-            vm((4 * QBLOCKS, HALF, LANES), F32),
+            vm((4 * QBLOCKS, HALF, LANES), BF),
+            vm((3 * RANK, RANK), BF),
+            vm((RANK, 1024), F32),
             vm((2, RANK, RANK), F32),
             vm((RANK, RANK), F32),
             dma((6,)),

time: 95.2 us -> 94.8 us (level)
  no operation moved by 1% of the time
where the time goes in v7:
time: 94.8 us; the launch traced here: 94.7 us
  Pallas kernels  94 us (99%)
    pallas_call x1, Pallas kernels, on_device(): pl.pallas_call(kernel, out_shape=pltpu.VMEM((RANK, 1024), F32), in_specs=...  94 us

profile of v7, /device:TPU:1, one launch (start us, length us, event | category | flops | bytes accessed | tf_op | source)
XLA Modules:
  0.0 94.7 jit_solution(15272971089318439048)
XLA Ops:
  0.0 94.0 %powersgd.1 = f32[32,1024]{1,0:T(8,128)S(1)} custom-call(bf16[2,8,16,3584]{3,2,1,0:T(8,128)(2,1)} %bitcast.1, bf16[2,16,8192]{2,1,0:T(8,128)(2,1)} %cot.1, f32[32,1024]{1,0:T(8,128)} %startq.1), custom_call_target="tpu_custom_call" | custom-call | tf_op jit(solution)/shard_map/powersgd/pallas_call | solution.py:411
  94.0 0.7 copy.5

commit v8 on v6

--- a/solution.py
+++ b/solution.py
@@ -101,7 +101,7 @@
 def kernel(
     hid, cot, startq, out,
     hbuf, cbuf, tbuf, qf, qsrc, qgat, sk0, sk1, ptsrc, ptrs, pt, mx, part0, gram0, gram1, wbuf,
-    zsrc, zrs, zall, minv, umat,
+    zsrc, zrs, zall, mparts, shifted, minv, umat,
     s_local, s_core, r_core, s_q, r_q, s_sk, r_sk, s_t, r_t, s_tc, r_tc, s_prs, r_prs, s_pag, r_pag,
     s_ptc, r_ptc, s_mx, r_mx, s_g, r_g, s_w, r_w, s_zrs, r_zrs, s_qag, r_qag,
 ):
@@ -355,7 +355,7 @@
 
         zrs[s, chip] = zsrc[s, q_mine]
         wait_bytes(zrs.at[s, pl.ds(0, CHIPS - 1)], r_zrs.at[s])
-        zall[z_mine] = sum_slots(zrs.at[s], CHIPS) * (1.0 / 64.0)
+        zall[z_mine] = (sum_slots(zrs.at[s], CHIPS) * (1.0 / 64.0)).astype(BF)
         tile = zall.at[z_mine]
         for d in NEAR:
             for core in (c, 1 - c) if d != (0, 0) else (1 - c,):
@@ -367,6 +367,13 @@
         if s == 1:
             shift = exact_dot(inner[:, RANK : 2 * RANK], qf[...])
         minv[s] = inverse_lower(inner)
+        rest = minv[s]
+        for n in range(3):
+            part = rest.astype(BF)
+            mparts[n * RANK : (n + 1) * RANK, :] = part
+            rest = rest - part.astype(F32)
+        if s == 1:
+            shifted[...] = exact_dot(minv[1], shift)
         wait_bytes(zall.at[pl.ds(0, 15)], r_qag.at[s])
         value = jnp.concatenate(
             [
@@ -375,9 +382,10 @@
             ],
             axis=0,
         )
+        parts = dot(mparts[...], value)
+        value = parts[:RANK] + (parts[RANK : 2 * RANK] + parts[2 * RANK :])
         if s == 1:
-            value = value - shift
-        value = exact_dot(minv[s], value)
+            value = value - shifted[...]
         if s == 0:
             qf[...] = value
             rows = qf[pl.ds(pl.multiple_of(c * HALF, HALF), HALF), :].astype(BF)
@@ -426,7 +434,9 @@
             vm((NY, 8, LANES), F32),
             vm((2, QBLOCKS, HALF, LANES), BF),
             vm((2, CHIPS, HALF, LANES), BF),
-            vm((4 * QBLOCKS, HALF, LANES), F32),
+            vm((4 * QBLOCKS, HALF, LANES), BF),
+            vm((3 * RANK, RANK), BF),
+            vm((RANK, 1024), F32),
             vm((2, RANK, RANK), F32),
             vm((RANK, RANK), F32),
             dma((6,)),

time: 95.2 us -> 94.7 us (level)
  no operation moved by 1% of the time
where the time goes in v8:
time: 94.7 us; the launch traced here: 94.6 us
  Pallas kernels  93.9 us (99%)
    pallas_call x1, Pallas kernels, on_device(): pl.pallas_call(kernel, out_shape=pltpu.VMEM((RANK, 1024), F32), in_specs=...  93.9 us

profile of v8, /device:TPU:1, one launch (start us, length us, event | category | flops | bytes accessed | tf_op | source)
XLA Modules:
  0.0 94.6 jit_solution(167231549375086422)
XLA Ops:
  0.0 93.9 %powersgd.1 = f32[32,1024]{1,0:T(8,128)S(1)} custom-call(bf16[2,8,16,3584]{3,2,1,0:T(8,128)(2,1)} %bitcast.1, bf16[2,16,8192]{2,1,0:T(8,128)(2,1)} %cot.1, f32[32,1024]{1,0:T(8,128)} %startq.1), custom_call_target="tpu_custom_call" | custom-call | tf_op jit(solution)/shard_map/powersgd/pallas_call | solution.py:413
  93.9 0.7 copy.5

commit v9 on v8

--- a/solution.py
+++ b/solution.py
@@ -75,11 +75,14 @@
     )
 
 
+def sum_terms(terms):
+    while len(terms) > 1:
+        terms = [a + b for a, b in zip(terms[::2], terms[1::2])] + terms[len(terms) & ~1 :]
+    return terms[0]
+
+
 def sum_slots(ref, count):
-    terms = [ref[n].astype(F32) for n in range(count)]
-    while len(terms) > 1:
-        terms = [a + b for a, b in zip(terms[::2], terms[1::2])]
-    return terms[0]
+    return sum_terms([ref[n].astype(F32) for n in range(count)])
 
 
 def inverse_lower(gram):
@@ -170,10 +173,12 @@
         cols = pl.ds(pl.multiple_of(owner * 1024, 1024), 1024)
         return nt_dot(q_rows, cbuf[:, :, cols].reshape(RANK, 1024))
 
-    sketch = block_sketch(qsrc[...], y)
-    for n, k in sorted(enumerate(Y_ORDER), key=lambda e: min(e[1], NY - e[1])):
-        wait_bytes(qgat.at[n], r_q.at[n])
-        sketch = sketch + block_sketch(qgat[n], lax.rem(y - k + NY, NY))
+    terms = [block_sketch(qsrc[...], y)]
+    for some in ((1, 7, 2, 6), (3, 5, 4)):
+        for k in some:
+            wait_bytes(qgat.at[Y_ORDER.index(k)], r_q.at[Y_ORDER.index(k)])
+        terms += [block_sketch(qgat[Y_ORDER.index(k)], lax.rem(y - k + NY, NY)) for k in some]
+    sketch = sum_terms(terms)
     spot = lax.broadcasted_iota(jnp.int32, (RANK, LANES), 0) + RANK * lax.rem(y, 4)
     place = jnp.where(lax.broadcasted_iota(jnp.int32, (RANK, LANES), 1) == spot, 1.0, 0.0).astype(BF)
     sk0[y] = dot(sketch.astype(BF), place).astype(BF)
@@ -279,7 +284,6 @@
         mixed = [None] * used
         for step in PLANES_IN:
             n = lax.rem(z + step, NZ - 1)
-            first = pl.multiple_of(n * NX, NX)
             if step == 0:
 
                 @pl.when(pt_owner)
@@ -292,11 +296,15 @@
 
             else:
                 wait_bytes(pt.at[s, c, pl.ds(0, NX)], r_pag.at[s, n])
-            cols = pl.ds(pl.multiple_of(n * GROUP, GROUP), GROUP)
-            rows = jnp.concatenate([pt[s, c, first + g] for g in range(NX)], axis=1)
-            for j in range(used):
-                term = nt_dot(rows, hbuf[j, :, :, :, cols].reshape(256, GROUP))
-                mixed[j] = term if mixed[j] is None else mixed[j] + term
+            if step not in (5, 4):
+                continue
+            for late in PLANES_IN[:5] if step == 5 else PLANES_IN[5:]:
+                n = lax.rem(z + late, NZ - 1)
+                cols = pl.ds(pl.multiple_of(n * GROUP, GROUP), GROUP)
+                rows = jnp.concatenate([pt[s, c, n * NX + g] for g in range(NX)], axis=1)
+                for j in range(used):
+                    term = nt_dot(rows, hbuf[j, :, :, :, cols].reshape(256, GROUP))
+                    mixed[j] = term if mixed[j] is None else mixed[j] + term
         send(pt.at[s, c], pt.at[s, c], s_ptc.at[s], r_ptc.at[s], sib)
         sent(pt.at[s, 0], s_ptc.at[s])
         for j in range(used):
@@ -388,7 +396,7 @@
             value = value - shifted[...]
         if s == 0:
             qf[...] = value
-            rows = qf[pl.ds(pl.multiple_of(c * HALF, HALF), HALF), :].astype(BF)
+            rows = jnp.where(c == 0, value[:HALF], value[HALF:]).astype(BF)
             wait_bytes(tbuf.at[1, :, 0], r_tc.at[1])
             for j in range(2):
                 sk1[j, y] = nt_dot(rows, tbuf[j].reshape(256, 1024)).astype(BF)

time: 94.7 us -> 95.2 us (level)
  no operation moved by 1% of the time
where the time goes in v9:
time: 95.2 us; the launch traced here: 95.1 us
  Pallas kernels  94.4 us (99%)
    pallas_call x1, Pallas kernels, on_device(): pl.pallas_call(kernel, out_shape=pltpu.VMEM((RANK, 1024), F32), in_specs=...  94.4 us

profile of v9, /device:TPU:1, one launch (start us, length us, event | category | flops | bytes accessed | tf_op | source)
XLA Modules:
  0.0 95.1 jit_solution(9166960000589616947)
XLA Ops:
  0.0 94.4 %powersgd.1 = f32[32,1024]{1,0:T(8,128)S(1)} custom-call(bf16[2,8,16,3584]{3,2,1,0:T(8,128)(2,1)} %bitcast.1, bf16[2,16,8192]{2,1,0:T(8,128)(2,1)} %cot.1, f32[32,1024]{1,0:T(8,128)} %startq.1), custom_call_target="tpu_custom_call" | custom-call | tf_op jit(solution)/shard_map/powersgd/pallas_call | solution.py:421
  94.4 0.7 copy.5

commit v10 on v7

--- a/solution.py
+++ b/solution.py
@@ -100,7 +100,7 @@
 
 def kernel(
     hid, cot, startq, out,
-    hbuf, cbuf, tbuf, qf, qsrc, qgat, sk0, sk1, ptsrc, ptrs, pt, mx, part0, gram0, gram1, wbuf,
+    hbuf, cbuf, tbuf, qf, qsrc, qgat, sk0, sk1, ptsrc, ptrs, pt, mx0, mx1, gram0, gram1, wbuf,
     zsrc, zrs, zall, mparts, shifted, minv, umat,
     s_local, s_core, r_core, s_q, r_q, s_sk, r_sk, s_t, r_t, s_tc, r_tc, s_prs, r_prs, s_pag, r_pag,
     s_ptc, r_ptc, s_mx, r_mx, s_g, r_g, s_w, r_w, s_zrs, r_zrs, s_qag, r_qag,
@@ -219,18 +219,16 @@
             load_h[0].wait()
             wait_bytes(hbuf.at[0, :, 0], r_core.at[1])
         if s == 1:
-            wait_bytes(sk1.at[0, pl.ds(0, NY - 1)], r_sk.at[1])
-            part0[...] = dot(sum_slots(sk1.at[0], NY).astype(BF), hbuf[0].reshape(256, 3584))
             load_h[1].wait()
             wait_bytes(hbuf.at[1, :, 0], r_core.at[2])
-            wait_bytes(sk1.at[1, pl.ds(0, NY - 1)], r_sk.at[2])
-            left = sum_slots(sk1.at[1], NY).astype(BF)
+            wait_bytes(sk1.at[pl.ds(0, NY - 1)], r_sk.at[1])
+            left = jnp.concatenate([sum_slots(sk1.at[:, j], NY).astype(BF) for j in range(2)], axis=1)
         for step in PLANES_OUT:
             n = lax.rem(z + step, NZ - 1)
             cols = pl.ds(pl.multiple_of(n * GROUP, GROUP), GROUP)
-            part = dot(left, hbuf[s, :, :, :, cols].reshape(256, GROUP))
+            part = dot(left[:, :256], hbuf[0, :, :, :, cols].reshape(256, GROUP))
             if s == 1:
-                part = part + part0[:, cols]
+                part = part + dot(left[:, 256:], hbuf[1, :, :, :, cols].reshape(256, GROUP))
             part = part.astype(BF)
             for g in range(NX):
                 ptsrc[s, n * NX + g] = part[:, g * LANES : (g + 1) * LANES]
@@ -276,6 +274,7 @@
 
         sent(ptrs.at[s, pl.ds(0, CHIPS - 1)], s_pag.at[s], pt_owner)
 
+        mx = mx0 if s == 0 else mx1
         mixed = [None] * used
         for step in PLANES_IN:
             n = lax.rem(z + step, NZ - 1)
@@ -300,10 +299,10 @@
         send(pt.at[s, c], pt.at[s, c], s_ptc.at[s], r_ptc.at[s], sib)
         sent(pt.at[s, 0], s_ptc.at[s])
         for j in range(used):
-            mx[s, j, y] = mixed[j].astype(BF)
-            for k in Y_ORDER:
-                send(mx.at[s, j, y], mx.at[s, j, y], s_mx.at[s, j], r_mx.at[s, j], y_dev(k))
-            sent(mx.at[s, j, pl.ds(0, NY - 1)], s_mx.at[s, j])
+            mx[y, j] = mixed[j].astype(BF)
+        for k in Y_ORDER:
+            send(mx.at[y], mx.at[y], s_mx.at[s], r_mx.at[s], y_dev(k))
+        sent(mx.at[pl.ds(0, NY - 1)], s_mx.at[s])
 
         if s == 0:
             share_t(0)
@@ -332,9 +331,9 @@
         if s == 0:
             wait_bytes(tbuf.at[0, :, 0], r_tc.at[0])
         part = None
+        wait_bytes(mx.at[pl.ds(0, NY - 1)], r_mx.at[s])
         for j in range(used):
-            wait_bytes(mx.at[s, j, pl.ds(0, NY - 1)], r_mx.at[s, j])
-            term = dot(sum_slots(mx.at[s, j], NY).astype(BF), tbuf[j].reshape(256, 1024))
+            term = dot(sum_slots(mx.at[:, j], NY).astype(BF), tbuf[j].reshape(256, 1024))
             part = term if part is None else part + term
         part = part.astype(BF)
         for b in range(QBLOCKS):
@@ -389,10 +388,10 @@
             rows = qf[pl.ds(pl.multiple_of(c * HALF, HALF), HALF), :].astype(BF)
             wait_bytes(tbuf.at[1, :, 0], r_tc.at[1])
             for j in range(2):
-                sk1[j, y] = nt_dot(rows, tbuf[j].reshape(256, 1024)).astype(BF)
-                for k in Y_ORDER:
-                    send(sk1.at[j, y], sk1.at[j, y], s_sk.at[1 + j], r_sk.at[1 + j], y_dev(k))
-                sent(sk1.at[j, pl.ds(0, NY - 1)], s_sk.at[1 + j])
+                sk1[y, j] = nt_dot(rows, tbuf[j].reshape(256, 1024)).astype(BF)
+            for k in Y_ORDER:
+                send(sk1.at[y], sk1.at[y], s_sk.at[1], r_sk.at[1], y_dev(k))
+            sent(sk1.at[pl.ds(0, NY - 1)], s_sk.at[1])
             wbuf[y] = pack(exact_nt_dot(value, jnp.concatenate([value] * 4, axis=0)), 8)
             for k in Y_ORDER:
                 send(wbuf.at[y], wbuf.at[y], s_w, r_w, y_dev(k))
@@ -421,12 +420,12 @@
             vm((HALF, 1024), BF),
             vm((NY - 1, HALF, 1024), BF),
             vm((NY, HALF, LANES), BF),
-            vm((2, NY, HALF, 256), BF),
+            vm((NY, 2, HALF, 256), BF),
             vm((2, TILES, HALF, LANES), BF),
             vm((2, CHIPS, HALF, LANES), BF),
             vm((2, 2, TILES, HALF, LANES), BF),
-            vm((2, 2, NY, HALF, 256), BF),
-            vm((HALF, 3584), F32),
+            vm((NY, 1, HALF, 256), BF),
+            vm((NY, 2, HALF, 256), BF),
             vm((NY, 8, LANES), F32),
             vm((NY, 16, LANES), F32),
             vm((NY, 8, LANES), F32),
@@ -440,13 +439,13 @@
             dma((6,)),
             dma((3,)), dma((3,)),
             dma, dma((NY - 1,)),
-            dma((3,)), dma((3,)),
+            dma((2,)), dma((2,)),
             dma((2,)), dma((2,)),
             dma((2,)), dma((2,)),
             dma((2,)), dma((2,)),
             dma((2,)), dma((2, NZ - 1)),
             dma((2,)), dma((2,)),
-            dma((2, 2)), dma((2, 2)),
+            dma((2,)), dma((2,)),
             dma((2,)), dma((2,)),
             dma, dma,
             dma((2,)), dma((2,)),

time: 94.8 us -> 95.2 us (level)
  no operation moved by 1% of the time
where the time goes in v10:
time: 95.2 us; the launch traced here: 95.1 us
  Pallas kernels  94.4 us (99%)
    pallas_call x1, Pallas kernels, on_device(): pl.pallas_call(kernel, out_shape=pltpu.VMEM((RANK, 1024), F32), in_specs=...  94.4 us

profile of v10, /device:TPU:1, one launch (start us, length us, event | category | flops | bytes accessed | tf_op | source)
XLA Modules:
  0.0 95.1 jit_solution(17250804397407302597)
XLA Ops:
  0.0 94.4 %powersgd.1 = f32[32,1024]{1,0:T(8,128)S(1)} custom-call(bf16[2,8,16,3584]{3,2,1,0:T(8,128)(2,1)} %bitcast.1, bf16[2,16,8192]{2,1,0:T(8,128)(2,1)} %cot.1, f32[32,1024]{1,0:T(8,128)} %startq.1), custom_call_target="tpu_custom_call" | custom-call | tf_op jit(solution)/shard_map/powersgd/pallas_call | solution.py:410
  94.4 0.7 copy.5

commit v11 on v7

--- a/solution.py
+++ b/solution.py
@@ -155,25 +155,29 @@
     load_h[0].start()
     load_h[1].start()
     load_q.wait()
-    qsrc[...] = qf[pl.ds(pl.multiple_of(c * HALF, HALF), HALF), :].astype(BF)
+    for part in range(2):
+        own_rows = pl.ds(pl.multiple_of(c * HALF, HALF), HALF)
+        qsrc[part] = qf[own_rows, part * 512 : (part + 1) * 512].astype(BF)
     pl.semaphore_wait(bar, NY - 1 + CHIPS - 1 + len(NEAR))
 
-    for n, k in enumerate(Y_ORDER):
-        send(qsrc, qgat.at[n], s_q, r_q.at[n], y_dev(k))
+    for part in range(2):
+        for n, k in enumerate(Y_ORDER):
+            send(qsrc.at[part], qgat.at[n, part], s_q, r_q.at[n, part], y_dev(k))
     sent(qgat, s_q)
     send(cot.at[0], cbuf.at[c], s_core.at[0], r_core.at[0], sib)
     sent(cbuf.at[0], s_core.at[0])
     load_c.wait()
     wait_bytes(cbuf.at[0], r_core.at[0])
 
-    def block_sketch(q_rows, owner):
-        cols = pl.ds(pl.multiple_of(owner * 1024, 1024), 1024)
-        return nt_dot(q_rows, cbuf[:, :, cols].reshape(RANK, 1024))
-
-    sketch = block_sketch(qsrc[...], y)
-    for n, k in sorted(enumerate(Y_ORDER), key=lambda e: min(e[1], NY - e[1])):
-        wait_bytes(qgat.at[n], r_q.at[n])
-        sketch = sketch + block_sketch(qgat[n], lax.rem(y - k + NY, NY))
+    def block_sketch(q_rows, owner, part):
+        cols = pl.ds(pl.multiple_of(owner * 1024 + part * 512, 512), 512)
+        return nt_dot(q_rows, cbuf[:, :, cols].reshape(RANK, 512))
+
+    sketch = block_sketch(qsrc[0], y, 0) + block_sketch(qsrc[1], y, 1)
+    for part in range(2):
+        for n, k in sorted(enumerate(Y_ORDER), key=lambda e: min(e[1], NY - e[1])):
+            wait_bytes(qgat.at[n, part], r_q.at[n, part])
+            sketch = sketch + block_sketch(qgat[n, part], lax.rem(y - k + NY, NY), part)
     spot = lax.broadcasted_iota(jnp.int32, (RANK, LANES), 0) + RANK * lax.rem(y, 4)
     place = jnp.where(lax.broadcasted_iota(jnp.int32, (RANK, LANES), 1) == spot, 1.0, 0.0).astype(BF)
     sk0[y] = dot(sketch.astype(BF), place).astype(BF)
@@ -418,8 +422,8 @@
             vm((2, 16, 8192), BF),
             vm((2, NY, 2, 16, 1024), BF),
             vm((RANK, 1024), F32),
-            vm((HALF, 1024), BF),
-            vm((NY - 1, HALF, 1024), BF),
+            vm((2, HALF, 512), BF),
+            vm((NY - 1, 2, HALF, 512), BF),
             vm((NY, HALF, LANES), BF),
             vm((2, NY, HALF, 256), BF),
             vm((2, TILES, HALF, LANES), BF),
@@ -439,7 +443,7 @@
             vm((RANK, RANK), F32),
             dma((6,)),
             dma((3,)), dma((3,)),
-            dma, dma((NY - 1,)),
+            dma, dma((NY - 1, 2)),
             dma((3,)), dma((3,)),
             dma((2,)), dma((2,)),
             dma((2,)), dma((2,)),

time: 94.8 us -> 94.3 us (level)
  no operation moved by 1% of the time
where the time goes in v11:
time: 94.3 us; the launch traced here: 94.2 us
  Pallas kernels  93.5 us (99%)
    pallas_call x1, Pallas kernels, on_device(): pl.pallas_call(kernel, out_shape=pltpu.VMEM((RANK, 1024), F32), in_specs=...  93.5 us

profile of v11, /device:TPU:1, one launch (start us, length us, event | category | flops | bytes accessed | tf_op | source)
XLA Modules:
  0.0 94.2 jit_solution(8687531492859001723)
XLA Ops:
  0.0 93.5 %powersgd.1 = f32[32,1024]{1,0:T(8,128)S(1)} custom-call(bf16[2,8,16,3584]{3,2,1,0:T(8,128)(2,1)} %bitcast.1, bf16[2,16,8192]{2,1,0:T(8,128)(2,1)} %cot.1, f32[32,1024]{1,0:T(8,128)} %startq.1), custom_call_target="tpu_custom_call" | custom-call | tf_op jit(solution)/shard_map/powersgd/pallas_call | solution.py:415
  93.5 0.7 copy.5
